TPU v7x, 256 devices: a whole 4x4x8 slice. The times are simulated.
256 devices in a mesh: dp: 4 (over x), exp: 8 (over z), seq: 8 (over y, core).
Axes of the slice: x: 4, y: 4, z: 8, core: 2. Of those that a mesh axis runs over, the one named last changes fastest.
Arguments:
- query_rows: bfloat16 [32768, 5120], P(('dp', 'exp', 'seq')), may hold values from -22 to 22
- key_rows: bfloat16 [32768, 5120], P(('dp', 'exp', 'seq')), may hold values from -6 to 6
- value_rows: bfloat16 [32768, 5120], P(('dp', 'exp', 'seq')), may hold values from -6 to 6
- stream: bfloat16 [32768, 5120], P(('dp', 'exp', 'seq')), may hold values from -32 to 32
- shared_basis: bfloat16 [5120, 1024], P('seq'), may hold values from -0.078125 to 0.078125
- expert_gate_up: bfloat16 [128, 1024, 256], P(('exp', 'seq')), may hold values from -0.1875 to 0.1875
- expert_down: bfloat16 [128, 128, 5120], P(('exp', 'seq')), may hold values from -0.5 to 0.5
- attn_gate: bfloat16 [32, 5120], P(('dp', 'exp')), may hold values from 0.5 to 1.5
- ffn_scale: bfloat16 [32, 5120], P(('dp', 'exp')), may hold values from 0.5 to 1.5
- ffn_gate: bfloat16 [32, 5120], P(('dp', 'exp')), may hold values from 0.5 to 1.5
- expert_ids: int32 [32768, 2], P(('dp', 'exp', 'seq')), may hold values from 0 to 127, all different within a row; in each aligned block of 128 rows (0 to 127, 128 to 255, ...) at most 4 rows name the same one
- route_weights: float32 [32768, 2], P(('dp', 'exp', 'seq')), may hold values from 0.2 to 1
Outputs:
- output: bfloat16 [32768, 5120], P(('dp', 'exp', 'seq'))
Inputs may be any that keep to these rules, and one draw needn't show every extreme that they name: `expert_ids`: the two experts of a token differ. Among the 128 tokens of one device no expert is named more than 4 times, and in some blocks one is named exactly 4 times; a token's slot at an expert is the number of earlier (token, k) entries of its device, in row-major order, that name the same expert.
All inputs are finite; a program needn't handle non-finite values.
Results may differ from a plain program's by a relative error of at most 0.0051.
Values may be sent and summed in bfloat16 or wider, within the bound.
A program may use at most 128 MiB of HBM per device.

v0:
```python
import functools
import math

import jax
import jax.numpy as jnp
from jax import lax
from jax.experimental import pallas as pl
from jax.experimental.pallas import tpu as pltpu
from jax.sharding import PartitionSpec as P

HEAD_DIM = 128
LANES = 128
MESH = pl.DeviceIdType.MESH
epsilon = 1e-06
CAP = 4


def block_kernel(
    query_ref,
    key_ref,
    value_ref,
    stream_ref,
    down_ref,
    gate_up_ref,
    basis_ref,
    attn_gate_ref,
    ffn_scale_ref,
    ffn_gate_ref,
    info_ref,
    output_ref,
    kv_in,
    qs_in,
    stream_own,
    att_out,
    attended,
    modulated,
    partial,
    own_part,
    core_send,
    core_recv,
    part_send,
    part_recv,
    out_rows,
    near_rows,
    slot_rows,
    gate_up,
    hidden,
    hidden_all,
    weights,
    slot_out,
    mix_out,
    mix_in,
    info_y,
    info_z,
    info_x,
    kv_sem,
    qs_sem,
    own_sem,
    info_sem,
    near_w_sem,
    ring_sem,
    pair_w_sem,
    gate_up_sem,
    core_sem,
    part_sem,
    att_sem,
    near_sem,
    slot_sem,
    hid_sem,
    mix_sem,
    sent,
):
    x_count, z_count, s_count = (lax.axis_size(name) for name in ("dp", "exp", "seq"))
    y_count = s_count // 2
    x, z, s = (lax.axis_index(name) for name in ("dp", "exp", "seq"))
    y, c = s // 2, s % 2
    other_c = 1 - c
    pair = 2 * y + other_c
    tok_rows, model_width = attended.shape
    head_cols = kv_in.shape[2]
    heads_here = head_cols // HEAD_DIM
    cols = weights.shape[4]
    rank = near_rows.shape[2]
    slots = 4 * CAP
    quarter = model_width // x_count

    def remote(src, dst, send_sem, recv_sem, device):
        return pltpu.make_async_remote_copy(
            src_ref=src,
            dst_ref=dst,
            send_sem=send_sem,
            recv_sem=recv_sem,
            device_id=device,
            device_id_type=MESH,
        )

    def wait_bytes(ref, sem):
        pltpu.make_async_copy(ref, ref, sem).wait()

    def first_column(y_to):
        return pl.multiple_of(x * quarter + (y_to // 2) * head_cols + (y_to % 2) * 256, LANES)

    def near_order(step):
        return lax.rem(1 + 2 * step - 3 * (step // 2), 4)

    barrier = pltpu.get_barrier_semaphore()

    def greet(device):
        pl.semaphore_signal(barrier, inc=1, device_id=device, device_id_type=MESH)

    def greet_seq(step, carry):
        greet({"seq": lax.rem(s + step, s_count)})
        return carry

    def greet_z(step, carry):
        greet({"exp": lax.rem(z + step, z_count)})
        return carry

    def greet_x(step, carry):
        greet({"dp": lax.rem(x + step, x_count)})

        def greet_xy(y_step, inner):
            greet(
                {
                    "dp": lax.rem(x + step, x_count),
                    "seq": 2 * lax.rem(y + y_step, y_count) + c,
                }
            )
            return inner

        return lax.fori_loop(1, y_count, greet_xy, carry)

    lax.fori_loop(1, s_count, greet_seq, 0)
    lax.fori_loop(1, z_count, greet_z, 0)
    lax.fori_loop(1, x_count, greet_x, 0)

    my_rows = pl.ds(pl.multiple_of(s * tok_rows, tok_rows), tok_rows)
    my_cols = pl.ds(pl.multiple_of(s * head_cols, head_cols), head_cols)
    kv_refs = (key_ref, value_ref)
    qs_refs = (query_ref, stream_ref)
    for which in range(2):
        pltpu.make_async_copy(
            kv_refs[which].at[:, my_cols], kv_in.at[which, my_rows, :], kv_sem
        ).start()
        pltpu.make_async_copy(
            qs_refs[which].at[:, my_cols], qs_in.at[s, which], qs_sem.at[s]
        ).start()
        pltpu.make_async_copy(
            down_ref.at[which, :, pl.ds(first_column(y), cols)],
            weights.at[c, z, y, pl.ds(which * LANES, LANES), :],
            near_w_sem,
        ).start()
    pltpu.make_async_copy(gate_up_ref, gate_up.at[c], gate_up_sem.at[0]).start()
    pltpu.make_async_copy(stream_ref, stream_own, own_sem).start()
    pltpu.make_async_copy(info_ref, info_y.at[y], info_sem.at[0]).start()

    pl.semaphore_wait(barrier, s_count - 1 + z_count - 1 + (x_count - 1) * y_count)

    def near_first(step, carry):
        y_to = lax.rem(y + near_order(step), y_count)
        device = {"seq": 2 * y_to + c}
        remote(info_ref, info_y.at[y], sent.at[0], info_sem.at[0], device).start()
        for which in range(2):
            remote(
                down_ref.at[which, :, pl.ds(first_column(y_to), cols)],
                weights.at[c, z, y, pl.ds(which * LANES, LANES), :],
                sent.at[1],
                near_w_sem,
                device,
            ).start()
        return carry

    lax.fori_loop(0, y_count - 1, near_first, 0)

    def send_parts(refs, slot_of, sem, send_sem):
        def one_chip(step, carry):
            y_to = lax.rem(y + near_order(step), y_count)

            def one_core(core, inner):
                s_to = 2 * y_to + core

                @pl.when(s_to != s)
                def _send():
                    columns = pl.ds(pl.multiple_of(s_to * head_cols, head_cols), head_cols)
                    for which in range(2):
                        remote(
                            refs[which].at[:, columns], slot_of(which), send_sem, sem, {"seq": s_to}
                        ).start()

                return inner

            return lax.fori_loop(0, 2, one_core, carry)

        lax.fori_loop(0, y_count, one_chip, 0)

    send_parts(kv_refs, lambda which: kv_in.at[which, my_rows, :], kv_sem, sent.at[2])
    send_parts(qs_refs, lambda which: qs_in.at[s, which], qs_sem.at[s], sent.at[3])
    remote(gate_up_ref, gate_up.at[c], sent.at[4], gate_up_sem.at[1], {"seq": pair}).start()

    wait_bytes(info_y, info_sem.at[0])
    pltpu.make_async_copy(info_y, info_z.at[z], info_sem.at[1]).start()
    pltpu.make_async_copy(info_y, info_x.at[x], info_sem.at[2]).start()

    def info_to_z(step, carry):
        remote(
            info_y,
            info_z.at[z],
            sent.at[5],
            info_sem.at[1],
            {"exp": lax.rem(z + step, z_count)},
        ).start()
        return carry

    def info_to_x(step, carry):
        remote(
            info_y,
            info_x.at[x],
            sent.at[6],
            info_sem.at[2],
            {"dp": lax.rem(x + step, x_count)},
        ).start()
        return carry

    lax.fori_loop(1, z_count, info_to_z, 0)
    lax.fori_loop(1, x_count, info_to_x, 0)

    def pass_on(block, up, down):
        held = weights.at[c, block]
        if up is not None:

            @pl.when(up)
            def _up():
                remote(
                    held,
                    held,
                    sent.at[7],
                    ring_sem.at[block],
                    {"exp": lax.rem(z + 1, z_count)},
                ).start()

        if down is not None:

            @pl.when(down)
            def _down():
                remote(
                    held,
                    held,
                    sent.at[7],
                    ring_sem.at[block],
                    {"exp": lax.rem(z + z_count - 1, z_count)},
                ).start()

        remote(held, held, sent.at[8], pair_w_sem, {"seq": pair}).start()

    always = z >= 0
    half = z_count // 2

    def ring_step(step):
        below = lax.rem(z + z_count - step, z_count)
        above = lax.rem(z + step, z_count)
        wait_bytes(weights.at[c, below], ring_sem.at[below])
        if step == half:
            pass_on(below, None, None)
            return
        pass_on(below, always if step < half - 1 else c == 0, None)
        wait_bytes(weights.at[c, above], ring_sem.at[above])
        pass_on(above, None, always if step < half - 1 else c == 1)

    wait_bytes(weights.at[c, z], near_w_sem)
    pass_on(z, always, always)
    ring_step(1)

    wait_bytes(kv_in, kv_sem)
    ring_step(2)

    length = s_count * tok_rows
    lane = lax.broadcasted_iota(jnp.int32, (length, HEAD_DIM), 1)
    ones_column = jnp.where(lane == 0, 1.0, 0.0).astype(jnp.bfloat16)
    exponent_scale = 1.0 / (math.sqrt(HEAD_DIM) * math.log(2.0))
    gate_row = attn_gate_ref[:, my_cols].astype(jnp.float32)
    scale_row = ffn_scale_ref[:, my_cols].astype(jnp.float32)
    two = 2 * tok_rows
    tail_lane = lax.broadcasted_iota(jnp.int32, (two, LANES), 1)

    def with_tail(values, square, tail):
        high = square.astype(jnp.bfloat16).astype(jnp.float32)
        extra = jnp.where(tail == 0, high, jnp.where(tail == 1, square - high, 0.0))
        return jnp.concatenate([values, extra], axis=1)

    def add_core_part(step):
        wait_bytes(core_recv.at[step], core_sem.at[step])
        total = own_part[step] + core_recv[step].astype(jnp.float32)
        square = total[:, rank : rank + 1] + total[:, rank + 1 : rank + 2]
        return total[:, :rank], square

    def send_part(step):
        values, square = add_core_part(step)
        part_send[step] = with_tail(values, square, tail_lane[:tok_rows]).astype(jnp.bfloat16)
        distance = near_order(step)
        y_to = lax.rem(y + y_count - distance, y_count)
        remote(
            part_send.at[step],
            part_recv.at[step],
            sent.at[10],
            part_sem,
            {"seq": 2 * y_to + c},
        ).start()

    def one_chip(step, carry):
        y_from = lax.rem(y + y_count - near_order(step), y_count)
        for core in range(2):
            wait_bytes(qs_in.at[2 * y_from + core], qs_sem.at[2 * y_from + core])
        both = pl.ds(2 * y_from, 2)
        square = jnp.zeros((two, 1), jnp.float32)
        for head in range(heads_here):
            part = slice(head * HEAD_DIM, (head + 1) * HEAD_DIM)
            scores = lax.dot_general(
                qs_in[both, 0, :, part].reshape(two, HEAD_DIM),
                kv_in[0, :, part],
                (((1,), (1,)), ((), ())),
                preferred_element_type=jnp.float32,
            )
            row_max = jnp.max(scores, axis=-1, keepdims=True)
            raised = jnp.exp2((scores - row_max) * exponent_scale).astype(jnp.bfloat16)
            value_ones = jnp.concatenate([kv_in[1, :, part], ones_column], axis=1)
            mixed = jnp.dot(raised, value_ones, preferred_element_type=jnp.float32)
            mixed = (mixed[:, :HEAD_DIM] / mixed[:, HEAD_DIM : HEAD_DIM + 1]).astype(jnp.bfloat16)
            att_out[both, :, part] = mixed.reshape(2, tok_rows, HEAD_DIM)
            residual = qs_in[both, 1, :, part].reshape(two, HEAD_DIM).astype(
                jnp.float32
            ) + gate_row[:, part] * mixed.astype(jnp.float32)
            modulated[:, part] = (residual * scale_row[:, part]).astype(jnp.bfloat16)
            square = square + jnp.sum(residual * residual, axis=1, keepdims=True)
        product = jnp.dot(modulated[...], basis_ref[...], preferred_element_type=jnp.float32)
        partial[...] = with_tail(product, square, tail_lane).reshape(partial.shape)
        own_part[step] = partial[c]
        core_send[step] = partial[other_c].astype(jnp.bfloat16)
        remote(
            core_send.at[step], core_recv.at[step], sent.at[9], core_sem.at[step], {"seq": pair}
        ).start()

        @pl.when(step > 0)
        def _previous():
            send_part(step - 1)

        return carry

    lax.fori_loop(0, 2, one_chip, 0)
    ring_step(3)
    lax.fori_loop(2, y_count, one_chip, 0)

    def send_attended(s_to, carry):
        @pl.when(s_to == s)
        def _keep():
            pltpu.make_async_copy(att_out.at[s_to], attended.at[:, my_cols], att_sem).start()

        @pl.when(s_to != s)
        def _send():
            remote(
                att_out.at[s_to], attended.at[:, my_cols], sent.at[11], att_sem, {"seq": s_to}
            ).start()

        return carry

    values, square = add_core_part(y_count - 1)
    wait_bytes(part_recv, part_sem)
    for step in range(y_count - 1):
        arrived = part_recv[step].astype(jnp.float32)
        values = values + arrived[:, :rank]
        square = square + arrived[:, rank : rank + 1] + arrived[:, rank + 1 : rank + 2]
    low_rank = (values / jnp.sqrt(square / model_width + epsilon)).astype(jnp.bfloat16)

    def pick_rows(y_to):
        row = lax.broadcasted_iota(jnp.int32, (z_count * slots, tok_rows), 0)
        slot_here = (((row // slots) * y_count + y_to) * slots + row % slots).astype(jnp.float32)
        pick = (slot_here == info_ref[0:1, :]) | (slot_here == info_ref[1:2, :])
        pick = jnp.where(pick, 1.0, 0.0).astype(jnp.bfloat16)
        return jnp.dot(pick, low_rank, preferred_element_type=jnp.float32).astype(jnp.bfloat16)

    for step in range(y_count - 1):
        y_to = lax.rem(y + near_order(step), y_count)
        out_rows[step] = pick_rows(y_to)
        remote(
            out_rows.at[step], near_rows.at[y], sent.at[12], near_sem.at[y], {"seq": 2 * y_to + c}
        ).start()
    near_rows[y] = pick_rows(y)

    lax.fori_loop(0, s_count, send_attended, 0)

    def forward_rows(step, carry):
        y_from = lax.rem(y + y_count - near_order(lax.rem(step + y_count - 1, y_count)), y_count)

        @pl.when(step > 0)
        def _arrive():
            wait_bytes(near_rows.at[y_from], near_sem.at[y_from])

        def to_z(z_step, inner):
            z_to = lax.rem(z + z_step, z_count)
            rows = pl.ds(pl.multiple_of(z_to * slots, slots), slots)
            remote(
                near_rows.at[y_from, rows, :],
                slot_rows.at[z, y_from],
                sent.at[13],
                slot_sem,
                {"exp": z_to},
            ).start()
            return inner

        own = pl.ds(pl.multiple_of(z * slots, slots), slots)
        pltpu.make_async_copy(near_rows.at[y_from, own, :], slot_rows.at[z, y_from], slot_sem).start()
        return lax.fori_loop(1, z_count, to_z, carry)

    lax.fori_loop(0, y_count, forward_rows, 0)

    wait_bytes(info_z, info_sem.at[1])
    wait_bytes(gate_up.at[c], gate_up_sem.at[0])
    wait_bytes(gate_up.at[other_c], gate_up_sem.at[1])
    sources = z_count * y_count
    rows_total = sources * slots
    named = info_z[...].reshape(sources, info_z.shape[2], tok_rows)
    place = lax.broadcasted_iota(jnp.int32, (sources, slots, tok_rows), 1)
    slot_here = (place + (z * y_count + y) * slots).astype(jnp.float32)
    weight = jnp.where(slot_here == named[:, 0:1, :], named[:, 2:3, :], 0.0) + jnp.where(
        slot_here == named[:, 1:2, :], named[:, 3:4, :], 0.0
    )
    weight = jnp.sum(weight, axis=2, keepdims=True).reshape(rows_total, 1)

    wait_bytes(slot_rows, slot_sem)
    rows = slot_rows[...].reshape(rows_total, rank)
    expert = lax.broadcasted_iota(jnp.int32, (rows_total, 1), 0) % slots // CAP
    both_halves = jnp.zeros((rows_total, gate_up.shape[3]), jnp.float32)
    for which in range(4):
        product = jnp.dot(
            rows, gate_up[which // 2, which % 2], preferred_element_type=jnp.float32
        )
        both_halves = jnp.where(expert == which, product, both_halves)
    gate, up = both_halves[:, :LANES], both_halves[:, LANES:]
    hidden[...] = (gate / (1.0 + jnp.exp(-gate)) * up * weight).astype(jnp.bfloat16)

    run = y_count * slots
    own_run = pl.ds(pl.multiple_of(z * run, run), run)

    def hidden_to_z(step, carry):
        z_to = lax.rem(z + step, z_count)
        remote(
            hidden.at[pl.ds(pl.multiple_of(z_to * run, run), run), :],
            hidden_all.at[y, x, own_run, :],
            sent.at[14],
            hid_sem.at[0],
            {"exp": z_to},
        ).start()
        return carry

    pltpu.make_async_copy(
        hidden.at[own_run, :], hidden_all.at[y, x, own_run, :], hid_sem.at[0]
    ).start()
    lax.fori_loop(1, z_count, hidden_to_z, 0)
    wait_bytes(hidden_all.at[y, x], hid_sem.at[0])

    def hidden_to_x(step, carry):
        held = hidden_all.at[y, x]
        remote(
            held, held, sent.at[15], hid_sem.at[1], {"dp": lax.rem(x + step, x_count)}
        ).start()
        return carry

    lax.fori_loop(1, x_count, hidden_to_x, 0)
    wait_bytes(hidden_all.at[y, pl.ds(0, x_count - 1)], hid_sem.at[1])

    def hidden_to_y(step, carry):
        held = hidden_all.at[y]
        y_to = lax.rem(y + near_order(step), y_count)
        remote(held, held, sent.at[16], hid_sem.at[2 + y], {"seq": 2 * y_to + c}).start()
        return carry

    lax.fori_loop(0, y_count - 1, hidden_to_y, 0)

    ring_step(half)
    wait_bytes(weights.at[other_c], pair_w_sem)
    wait_bytes(info_x, info_sem.at[2])

    group = x_count * y_count
    chip_rows = group * slots
    chip_expert = lax.broadcasted_iota(jnp.int32, (chip_rows, LANES), 0) % slots // CAP

    def down_chip(step, carry):
        y_from = lax.rem(y + y_count - near_order(lax.rem(step + y_count - 1, y_count)), y_count)

        @pl.when(step > 0)
        def _arrive():
            wait_bytes(hidden_all.at[y_from], hid_sem.at[2 + y_from])

        def down_one(z_from, inner):
            at = pl.ds(pl.multiple_of(z_from * run, run), run)
            held = jnp.concatenate(
                [hidden_all[y_from, x_from, at, :] for x_from in range(x_count)], axis=0
            )
            held = held.astype(jnp.float32)
            masked = [
                jnp.where(chip_expert == which, held, 0.0).astype(jnp.bfloat16)
                for which in range(4)
            ]
            product = jnp.dot(
                jnp.concatenate(masked[:2], axis=1),
                weights[0, z_from, y_from],
                preferred_element_type=jnp.float32,
            ) + jnp.dot(
                jnp.concatenate(masked[2:], axis=1),
                weights[1, z_from, y_from],
                preferred_element_type=jnp.float32,
            )
            to = pl.ds(pl.multiple_of((z_from * y_count + y_from) * slots, slots), slots)
            slot_out[:, to, :] = product.astype(jnp.bfloat16).reshape(group, slots, cols)
            return inner

        return lax.fori_loop(0, z_count, down_one, carry)

    lax.fori_loop(0, y_count, down_chip, 0)

    mine = x * y_count + y

    def mix_one(step, carry):
        x_to = lax.rem(x + (step + 1) // y_count, x_count)
        y_to = lax.rem(y + step + 1, y_count)
        to = x_to * y_count + y_to
        slot_iota = lax.broadcasted_iota(jnp.int32, (slot_out.shape[1], tok_rows), 0).astype(
            jnp.float32
        )
        named_here = info_x[x_to, y_to]
        pick = (slot_iota == named_here[0:1, :]) | (slot_iota == named_here[1:2, :])
        pick = jnp.where(pick, 1.0, 0.0).astype(jnp.bfloat16)
        mixed = lax.dot_general(
            pick, slot_out[to], (((0,), (0,)), ((), ())), preferred_element_type=jnp.float32
        )
        mix_out[to] = mixed.astype(jnp.bfloat16)

        @pl.when(to == mine)
        def _keep():
            pltpu.make_async_copy(mix_out.at[to], mix_in.at[mine], mix_sem).start()

        @pl.when(to != mine)
        def _send():
            remote(
                mix_out.at[to],
                mix_in.at[mine],
                sent.at[17],
                mix_sem,
                {"dp": x_to, "seq": 2 * y_to + c},
            ).start()

        return carry

    lax.fori_loop(0, group, mix_one, 0)

    wait_bytes(stream_own, own_sem)
    wait_bytes(attended, att_sem)
    wait_bytes(mix_in, mix_sem)
    for block in range(s_count):
        part = slice(block * head_cols, (block + 1) * head_cols)
        mixed = jnp.concatenate([mix_in[2 * block], mix_in[2 * block + 1, :, LANES:]], axis=1)
        residual = stream_own[:, part].astype(jnp.float32) + attn_gate_ref[:, part].astype(
            jnp.float32
        ) * attended[:, part].astype(jnp.float32)
        output_ref[:, part] = (
            residual + ffn_gate_ref[:, part].astype(jnp.float32) * mixed.astype(jnp.float32)
        ).astype(jnp.bfloat16)

    wait_bytes(info_y.at[pl.ds(0, y_count - 1)], sent.at[0])
    wait_bytes(weights.at[0, 0, pl.ds(0, y_count - 1)], sent.at[1])
    wait_bytes(kv_in.at[:, pl.ds(0, (s_count - 1) * tok_rows), :], sent.at[2])
    wait_bytes(qs_in.at[pl.ds(0, s_count - 1)], sent.at[3])
    wait_bytes(gate_up.at[0], sent.at[4])
    wait_bytes(info_z.at[pl.ds(0, z_count - 1)], sent.at[5])
    wait_bytes(info_x.at[pl.ds(0, x_count - 1)], sent.at[6])
    wait_bytes(weights.at[0, pl.ds(0, z_count - 1)], sent.at[7])
    wait_bytes(weights.at[0], sent.at[8])
    wait_bytes(core_send, sent.at[9])
    wait_bytes(part_send, sent.at[10])
    wait_bytes(att_out.at[pl.ds(0, s_count - 1)], sent.at[11])
    wait_bytes(out_rows, sent.at[12])
    wait_bytes(slot_rows.at[pl.ds(0, z_count - 1)], sent.at[13])
    wait_bytes(hidden.at[pl.ds(0, (z_count - 1) * run), :], sent.at[14])
    wait_bytes(hidden_all.at[0, pl.ds(0, x_count - 1)], sent.at[15])
    wait_bytes(hidden_all.at[pl.ds(0, y_count - 1)], sent.at[16])
    wait_bytes(mix_out.at[pl.ds(0, group - 1)], sent.at[17])


def on_device(
    query_rows,
    key_rows,
    value_rows,
    stream,
    shared_basis,
    expert_gate_up,
    expert_down,
    attn_gate,
    ffn_scale,
    ffn_gate,
    expert_ids,
    route_weights,
):
    x_count, z_count, s_count = (lax.axis_size(name) for name in ("dp", "exp", "seq"))
    y_count = s_count // 2
    tok_rows, model_width = stream.shape
    experts_here, hidden_cols, _ = expert_down.shape
    expert_total = z_count * s_count * experts_here
    rank = shared_basis.shape[1]
    head_cols = model_width // s_count
    cols = 384
    slots = 4 * CAP
    length = s_count * tok_rows
    group = x_count * y_count

    flat_ids = expert_ids.T.reshape(2 * tok_rows)
    one_hot = (flat_ids[:, None] == jnp.arange(expert_total, dtype=jnp.int32)[None, :]).astype(
        jnp.bfloat16
    )
    entry = jnp.arange(2 * tok_rows, dtype=jnp.int32)
    order = 2 * (entry % tok_rows) + entry // tok_rows
    before = (order[None, :] < order[:, None]).astype(jnp.bfloat16)
    same = jnp.dot(before, one_hot, preferred_element_type=jnp.float32)
    slot_rank = jnp.sum(same * one_hot.astype(jnp.float32), axis=1)
    slot_ids = flat_ids.astype(jnp.float32) * CAP + slot_rank
    info = jnp.concatenate(
        [
            slot_ids.reshape(2, tok_rows),
            route_weights.T,
            jnp.zeros((4, tok_rows), jnp.float32),
        ],
        axis=0,
    )

    vmem = pl.BlockSpec(memory_space=pltpu.VMEM)
    anywhere = pl.BlockSpec(memory_space=pl.ANY)
    bf16, f32 = jnp.bfloat16, jnp.float32
    wide = rank + LANES
    dma = pltpu.SemaphoreType.DMA
    return pl.pallas_call(
        block_kernel,
        out_shape=jax.ShapeDtypeStruct((tok_rows, model_width), bf16),
        in_specs=[anywhere] * 6 + [vmem] * 5,
        out_specs=vmem,
        scratch_shapes=[
            pltpu.VMEM((2, length, head_cols), bf16),
            pltpu.VMEM((s_count, 2, tok_rows, head_cols), bf16),
            pltpu.VMEM((tok_rows, model_width), bf16),
            pltpu.VMEM((s_count, tok_rows, head_cols), bf16),
            pltpu.VMEM((tok_rows, model_width), bf16),
            pltpu.VMEM((2 * tok_rows, head_cols), bf16),
            pltpu.VMEM((2, tok_rows, wide), f32),
            pltpu.VMEM((y_count, tok_rows, wide), f32),
            pltpu.VMEM((y_count, tok_rows, wide), bf16),
            pltpu.VMEM((y_count, tok_rows, wide), bf16),
            pltpu.VMEM((y_count - 1, tok_rows, wide), bf16),
            pltpu.VMEM((y_count - 1, tok_rows, wide), bf16),
            pltpu.VMEM((y_count - 1, z_count * slots, rank), bf16),
            pltpu.VMEM((y_count, z_count * slots, rank), bf16),
            pltpu.VMEM((z_count, y_count, slots, rank), bf16),
            pltpu.VMEM((2,) + expert_gate_up.shape, bf16),
            pltpu.VMEM((z_count * y_count * slots, hidden_cols), bf16),
            pltpu.VMEM((y_count, x_count, z_count * y_count * slots, hidden_cols), bf16),
            pltpu.VMEM((2, z_count, y_count, experts_here * hidden_cols, cols), bf16),
            pltpu.VMEM((group, z_count * y_count * slots, cols), bf16),
            pltpu.VMEM((group, tok_rows, cols), bf16),
            pltpu.VMEM((group, tok_rows, cols), bf16),
            pltpu.VMEM((y_count, 8, tok_rows), f32),
            pltpu.VMEM((z_count, y_count, 8, tok_rows), f32),
            pltpu.VMEM((x_count, y_count, 8, tok_rows), f32),
            dma,
            dma((s_count,)),
            dma,
            dma((3,)),
            dma,
            dma((z_count,)),
            dma,
            dma((2,)),
            dma((y_count,)),
            dma,
            dma,
            dma((y_count,)),
            dma,
            dma((2 + y_count,)),
            dma,
            dma((18,)),
        ],
        compiler_params=pltpu.CompilerParams(
            collective_id=0, has_side_effects=True, vmem_limit_bytes=62 * 1024 * 1024
        ),
        name="block",
    )(
        query_rows,
        key_rows,
        value_rows,
        stream,
        expert_down,
        expert_gate_up,
        shared_basis,
        attn_gate,
        ffn_scale,
        ffn_gate,
        info,
    )


def solution(mesh):
    in_specs = (
        P(("dp", "exp", "seq"), None),
        P(("dp", "exp", "seq"), None),
        P(("dp", "exp", "seq"), None),
        P(("dp", "exp", "seq"), None),
        P("seq", None),
        P(("exp", "seq"), None, None),
        P(("exp", "seq"), None, None),
        P(("dp", "exp"), None),
        P(("dp", "exp"), None),
        P(("dp", "exp"), None),
        P(("dp", "exp", "seq"), None),
        P(("dp", "exp", "seq"), None),
    )
    out_specs = P(("dp", "exp", "seq"), None)
    return jax.shard_map(
        on_device, mesh=mesh, in_specs=in_specs, out_specs=out_specs, check_vma=False
    )
```

profile of v0, /device:TPU:64, one launch (start us, length us, event | category | flops | bytes accessed | tf_op | source)
XLA Modules:
  0.0 202.2 jit_solution(9509667959154050524)
XLA Ops:
  0.0 0.1 pad.2.clone
  0.1 1.1 fusion
  1.1 0.7 bitcast_add_fusion
  1.8 1.3 maximum_maximum_fusion.info_ref
  3.2 196.6 %block.1 = bf16[128,5120]{1,0:T(8,128)(2,1)} custom-call(bf16[128,5120]{1,0:T(8,128)(2,1)} %query_ref.1, bf16[128,5120]{1,0:T(8,128)(2,1)} %key_ref.1, bf16[128,5120]{1,0:T(8,128)(2,1)} %value_ref.1, bf16[128,5120]{1,0:T(8,128)(2,1)} %stream_ref.1, bf16[2,128,5120]{2,1,0:T(8,128)(2,1)} %down_ref.1, bf16[2,1024,256]{2,1,0:T(8,128)(2,1)} %gate_up_ref.1, ...), custom_call_target="tpu_custom_call" | custom-call | tf_op jit(solution)/shard_map/block/pallas_call | solution.py:638
  199.7 2.5 %copy.14 = bf16[128,5120]{1,0:T(8,128)(2,1)} copy(bf16[128,5120]{1,0:T(8,128)(2,1)} %block.1) | data formatting | bytes 2621440
  (2 shorter events, 0.0 us)
where the time goes:
time: 202 us
  Pallas kernels  197 us (98%)
  local copies, waits for them, and re-layouts  2.54 us (1%)
  other arithmetic  2.03 us (1%)
    pallas_call x1, Pallas kernels, on_device(): pl.pallas_call(block_kernel, out_shape=jax.ShapeDtypeStruct((tok_rows, mo...  197 us

commit v1 on v0

v1 whole, which is shorter than its diff:
```python
import functools
import math

import jax
import jax.numpy as jnp
from jax import lax
from jax.experimental import pallas as pl
from jax.experimental.pallas import tpu as pltpu
from jax.sharding import PartitionSpec as P

HEAD_DIM = 128
LANES = 128
MESH = pl.DeviceIdType.MESH
epsilon = 1e-06
CAP = 4


def block_kernel(
    query_ref,
    key_ref,
    value_ref,
    stream_ref,
    down_ref,
    gate_up_ref,
    basis_ref,
    attn_gate_ref,
    ffn_scale_ref,
    ffn_gate_ref,
    ids_ref,
    route_ref,
    output_ref,
    kv_in,
    qs_in,
    stream_own,
    att_out,
    attended,
    modulated,
    partial,
    own_part,
    core_send,
    core_recv,
    part_send,
    part_recv,
    out_rows,
    near_rows,
    slot_rows,
    gate_up,
    hidden_all,
    weights,
    slot_out,
    mix_out,
    mix_in,
    info_own,
    info_y,
    info_x,
    kv_sem,
    qs_sem,
    batch_sem,
    own_sem,
    info_sem,
    near_w_sem,
    ring_sem,
    pair_w_sem,
    near_g_sem,
    ring_g_sem,
    pair_g_sem,
    core_sem,
    part_sem,
    att_sem,
    near_sem,
    slot_sem,
    hid_sem,
    hid_y_sem,
    hid_x_sem,
    mix_sem,
    sent,
):
    x_count, z_count, s_count = (lax.axis_size(name) for name in ("dp", "exp", "seq"))
    y_count = s_count // 2
    x, z, s = (lax.axis_index(name) for name in ("dp", "exp", "seq"))
    y, c = s // 2, s % 2
    other_c = 1 - c
    pair = 2 * y + other_c
    tok_rows, model_width = attended.shape
    head_cols = kv_in.shape[2]
    heads_here = head_cols // HEAD_DIM
    cols = weights.shape[4]
    rank = near_rows.shape[2]
    slots = 4 * CAP
    quarter = model_width // x_count

    def remote(src, dst, send_sem, recv_sem, device):
        return pltpu.make_async_remote_copy(
            src_ref=src,
            dst_ref=dst,
            send_sem=send_sem,
            recv_sem=recv_sem,
            device_id=device,
            device_id_type=MESH,
        )

    def wait_bytes(ref, sem):
        pltpu.make_async_copy(ref, ref, sem).wait()

    def first_column(y_to):
        return pl.multiple_of(x * quarter + (y_to // 2) * head_cols + (y_to % 2) * 256, LANES)

    def near_order(step):
        return step + step // 2 - 2 * (step // 3)

    barrier = pltpu.get_barrier_semaphore()

    def greet(device):
        pl.semaphore_signal(barrier, inc=1, device_id=device, device_id_type=MESH)

    def greet_seq(step, carry):
        greet({"seq": lax.rem(s + step, s_count)})
        return carry

    def greet_z(step, carry):
        greet({"exp": lax.rem(z + step, z_count)})
        return carry

    def greet_x(step, carry):
        greet({"dp": lax.rem(x + step, x_count)})

        def greet_xy(y_step, inner):
            greet(
                {
                    "dp": lax.rem(x + step, x_count),
                    "seq": 2 * lax.rem(y + y_step, y_count) + c,
                }
            )
            return inner

        return lax.fori_loop(1, y_count, greet_xy, carry)

    lax.fori_loop(1, s_count, greet_seq, 0)
    lax.fori_loop(1, z_count, greet_z, 0)
    lax.fori_loop(1, x_count, greet_x, 0)

    my_rows = pl.ds(pl.multiple_of(s * tok_rows, tok_rows), tok_rows)
    my_cols = pl.ds(pl.multiple_of(s * head_cols, head_cols), head_cols)
    kv_refs = (key_ref, value_ref)
    qs_refs = (query_ref, stream_ref)
    for which in range(2):
        pltpu.make_async_copy(
            kv_refs[which].at[:, my_cols], kv_in.at[which, my_rows, :], kv_sem
        ).start()
        pltpu.make_async_copy(
            qs_refs[which].at[:, my_cols], qs_in.at[s, which], qs_sem.at[s]
        ).start()
        pltpu.make_async_copy(
            down_ref.at[which, :, pl.ds(first_column(y), cols)],
            weights.at[c, z, y, pl.ds(which * LANES, LANES), :],
            near_w_sem,
        ).start()
    pltpu.make_async_copy(stream_ref, stream_own, own_sem).start()

    rank_part = rank // z_count
    twin = z - 2 * x

    @pl.when(z // 2 == x)
    def _own_gate_up():
        part = pl.ds(pl.multiple_of(z * rank_part, rank_part), rank_part)
        pltpu.make_async_copy(
            gate_up_ref.at[:, part, :], gate_up.at[c, z, twin], near_g_sem
        ).start()

    pl.semaphore_wait(barrier, s_count - 1 + z_count - 1 + (x_count - 1) * y_count)

    def near_first(step, carry):
        y_to = lax.rem(y + near_order(step), y_count)
        device = {"seq": 2 * y_to + c}
        for which in range(2):
            remote(
                down_ref.at[which, :, pl.ds(first_column(y_to), cols)],
                weights.at[c, z, y, pl.ds(which * LANES, LANES), :],
                sent.at[1],
                near_w_sem,
                device,
            ).start()
        return carry

    lax.fori_loop(1, y_count, near_first, 0)

    @pl.when(z // 2 == x)
    def _spread_gate_up():
        def to_z(step, carry):
            z_to = lax.rem(z + step, z_count)
            part = pl.ds(pl.multiple_of(z_to * rank_part, rank_part), rank_part)
            remote(
                gate_up_ref.at[:, part, :],
                gate_up.at[c, z_to, twin],
                sent.at[4],
                near_g_sem,
                {"exp": z_to},
            ).start()
            return carry

        lax.fori_loop(1, z_count, to_z, 0)


    def send_batch(refs, slot_of, sem, send_sem, distances):
        def one_copy(index, carry):
            s_to = 2 * lax.rem(y + distances[0] + 2 * (index % len(distances)), y_count) + (
                index // len(distances)
            )
            columns = pl.ds(pl.multiple_of(s_to * head_cols, head_cols), head_cols)
            for which in range(2):
                remote(
                    refs[which].at[:, columns], slot_of(which), send_sem, sem, {"seq": s_to}
                ).start()
            return carry

        if len(distances) == 2:
            columns = pl.ds(pl.multiple_of(pair * head_cols, head_cols), head_cols)
            for which in range(2):
                remote(
                    refs[which].at[:, columns], slot_of(which), send_sem, sem, {"seq": pair}
                ).start()
        lax.fori_loop(0, 2 * len(distances), one_copy, 0)

    batches = ((1, 3), (2,))

    def send_kv(batch):
        send_batch(
            kv_refs,
            lambda which: kv_in.at[which, my_rows, :],
            kv_sem,
            batch_sem.at[0, batch],
            batches[batch],
        )

    def send_qs(batch):
        send_batch(
            qs_refs,
            lambda which: qs_in.at[s, which],
            qs_sem.at[s],
            batch_sem.at[1, batch],
            batches[batch],
        )

    def batch_left(kind, batch):
        peers = 5 if batch == 0 else 2
        wait_bytes(qs_in.at[pl.ds(0, peers)], batch_sem.at[kind, batch])

    send_kv(0)

    entries = 2 * tok_rows
    experts = 4 * z_count * y_count
    ids_row = jnp.concatenate([ids_ref[0:1, :], ids_ref[1:2, :]], axis=1)
    named = lax.broadcasted_iota(jnp.int32, (experts, entries), 0) == ids_row
    entry = [lax.broadcasted_iota(jnp.int32, (entries, entries), axis) for axis in (0, 1)]
    entry = [2 * (one % tok_rows) + one // tok_rows for one in entry]
    before = jnp.where(entry[0] < entry[1], 1.0, 0.0).astype(jnp.bfloat16)
    counts = jnp.dot(
        jnp.where(named, 1.0, 0.0).astype(jnp.bfloat16), before, preferred_element_type=jnp.float32
    )
    slot_ids = (
        jnp.sum(jnp.where(named, counts, 0.0), axis=0, keepdims=True)
        + ids_row.astype(jnp.float32) * CAP
    )
    info_row = lax.broadcasted_iota(jnp.int32, info_own.shape, 0)
    info = jnp.where(info_row == 2, route_ref[0:1, :], 0.0)
    info = jnp.where(info_row == 3, route_ref[1:2, :], info)
    info = jnp.where(info_row == 0, slot_ids[:, :tok_rows], info)
    info_own[...] = jnp.where(info_row == 1, slot_ids[:, tok_rows:], info)
    pltpu.make_async_copy(info_own, info_y.at[y], info_sem.at[0]).start()

    def info_to_y(step, carry):
        y_to = lax.rem(y + step, y_count)
        remote(
            info_own, info_y.at[y], sent.at[0], info_sem.at[0], {"seq": 2 * y_to + c}
        ).start()
        return carry

    lax.fori_loop(1, y_count, info_to_y, 0)

    always = z >= 0
    half = z_count // 2

    def pass_on(buffer, sems, left_sem, pair_left, pair_sem, block, up, down):
        held = buffer.at[c, block]

        def pass_to(z_to):
            remote(held, held, left_sem, sems.at[block], {"exp": lax.rem(z_to, z_count)}).start()

        if up is not None:

            @pl.when(up)
            def _up():
                pass_to(z + 1)

        if down is not None:

            @pl.when(down)
            def _down():
                pass_to(z + z_count - 1)

        remote(held, held, pair_left, pair_sem, {"seq": pair}).start()

    def ring_step(ring, step):
        buffer, sems = ring[0], ring[1]
        below = lax.rem(z + z_count - step, z_count)
        above = lax.rem(z + step, z_count)
        wait_bytes(buffer.at[c, below], sems.at[below])
        if step == half:
            pass_on(*ring, below, None, None)
            return
        pass_on(*ring, below, always if step < half - 1 else c == 0, None)
        wait_bytes(buffer.at[c, above], sems.at[above])
        pass_on(*ring, above, None, always if step < half - 1 else c == 1)

    gate_ring = (gate_up, ring_g_sem, sent.at[13], sent.at[14], pair_g_sem)
    down_ring = (weights, ring_sem, sent.at[7], sent.at[8], pair_w_sem)

    wait_bytes(gate_up.at[c, z], near_g_sem)
    pass_on(*gate_ring, z, always, always)
    send_kv(1)
    ring_step(gate_ring, 1)
    wait_bytes(weights.at[c, z], near_w_sem)
    pass_on(*down_ring, z, always, always)
    batch_left(0, 0)
    send_qs(0)
    ring_step(gate_ring, 2)
    ring_step(gate_ring, 3)

    wait_bytes(info_y, info_sem.at[0])
    pltpu.make_async_copy(info_y, info_x.at[x], info_sem.at[1]).start()

    def info_to_x(step, carry):
        remote(
            info_y,
            info_x.at[x],
            sent.at[6],
            info_sem.at[1],
            {"dp": lax.rem(x + step, x_count)},
        ).start()
        return carry

    lax.fori_loop(1, x_count, info_to_x, 0)
    wait_bytes(kv_in, kv_sem)

    length = s_count * tok_rows
    lane = lax.broadcasted_iota(jnp.int32, (length, HEAD_DIM), 1)
    ones_column = jnp.where(lane == 0, 1.0, 0.0).astype(jnp.bfloat16)
    exponent_scale = 1.0 / (math.sqrt(HEAD_DIM) * math.log(2.0))
    gate_row = attn_gate_ref[:, my_cols].astype(jnp.float32)
    scale_row = ffn_scale_ref[:, my_cols].astype(jnp.float32)
    two = 2 * tok_rows
    tail_lane = lax.broadcasted_iota(jnp.int32, (two, LANES), 1)

    def with_tail(values, square, tail):
        high = square.astype(jnp.bfloat16).astype(jnp.float32)
        extra = jnp.where(tail == 0, high, jnp.where(tail == 1, square - high, 0.0))
        return jnp.concatenate([values, extra], axis=1)

    def add_core_part(step):
        wait_bytes(core_recv.at[step], core_sem.at[step])
        total = own_part[step] + core_recv[step].astype(jnp.float32)
        square = total[:, rank : rank + 1] + total[:, rank + 1 : rank + 2]
        return total[:, :rank], square

    def send_part(step):
        values, square = add_core_part(step)
        part_send[step - 1] = with_tail(values, square, tail_lane[:tok_rows]).astype(jnp.bfloat16)
        distance = near_order(step)
        y_to = lax.rem(y + y_count - distance, y_count)
        remote(
            part_send.at[step - 1],
            part_recv.at[step - 1],
            sent.at[10],
            part_sem,
            {"seq": 2 * y_to + c},
        ).start()

    def one_chip(step, carry):
        y_from = lax.rem(y + y_count - near_order(step), y_count)

        @pl.when(step > 1)
        def _previous():
            send_part(step - 1)

        for core in range(2):
            wait_bytes(qs_in.at[2 * y_from + core], qs_sem.at[2 * y_from + core])
        both = pl.ds(2 * y_from, 2)
        square = jnp.zeros((two, 1), jnp.float32)
        for head in range(heads_here):
            part = slice(head * HEAD_DIM, (head + 1) * HEAD_DIM)
            scores = lax.dot_general(
                qs_in[both, 0, :, part].reshape(two, HEAD_DIM),
                kv_in[0, :, part],
                (((1,), (1,)), ((), ())),
                preferred_element_type=jnp.float32,
            )
            row_max = jnp.max(scores, axis=-1, keepdims=True)
            raised = jnp.exp2((scores - row_max) * exponent_scale).astype(jnp.bfloat16)
            value_ones = jnp.concatenate([kv_in[1, :, part], ones_column], axis=1)
            mixed = jnp.dot(raised, value_ones, preferred_element_type=jnp.float32)
            mixed = (mixed[:, :HEAD_DIM] / mixed[:, HEAD_DIM : HEAD_DIM + 1]).astype(jnp.bfloat16)
            att_out[both, :, part] = mixed.reshape(2, tok_rows, HEAD_DIM)
            residual = qs_in[both, 1, :, part].reshape(two, HEAD_DIM).astype(
                jnp.float32
            ) + gate_row[:, part] * mixed.astype(jnp.float32)
            modulated[:, part] = (residual * scale_row[:, part]).astype(jnp.bfloat16)
            square = square + jnp.sum(residual * residual, axis=1, keepdims=True)
        product = jnp.dot(modulated[...], basis_ref[...], preferred_element_type=jnp.float32)
        partial[...] = with_tail(product, square, tail_lane).reshape(partial.shape)
        own_part[step] = partial[c]
        core_send[step] = partial[other_c].astype(jnp.bfloat16)
        remote(
            core_send.at[step], core_recv.at[step], sent.at[9], core_sem.at[step], {"seq": pair}
        ).start()
        return carry

    def after_chip(step, carry):
        one_chip(step, carry)

        @pl.when(step == 0)
        def _last_batch():
            ring_step(gate_ring, half)
            batch_left(0, 1)
            send_qs(1)

        @pl.when(step == 1)
        def _ring_one():
            ring_step(down_ring, 1)

        @pl.when(step == 2)
        def _ring_two():
            ring_step(down_ring, 2)

        return carry

    lax.fori_loop(0, y_count, after_chip, 0)
    send_part(y_count - 1)

    def send_attended(s_to, carry):
        @pl.when(s_to == s)
        def _keep():
            pltpu.make_async_copy(att_out.at[s_to], attended.at[:, my_cols], att_sem).start()

        @pl.when(s_to != s)
        def _send():
            remote(
                att_out.at[s_to], attended.at[:, my_cols], sent.at[11], att_sem, {"seq": s_to}
            ).start()

        return carry

    values, square = add_core_part(0)
    wait_bytes(part_recv, part_sem)
    for step in range(y_count - 1):
        arrived = part_recv[step].astype(jnp.float32)
        values = values + arrived[:, :rank]
        square = square + arrived[:, rank : rank + 1] + arrived[:, rank + 1 : rank + 2]
    low_rank = (values / jnp.sqrt(square / model_width + epsilon)).astype(jnp.bfloat16)

    def pick_rows(y_to):
        row = lax.broadcasted_iota(jnp.int32, (z_count * slots, tok_rows), 0)
        slot_here = (((row // slots) * y_count + y_to) * slots + row % slots).astype(jnp.float32)
        pick = (slot_here == info_own[0:1, :]) | (slot_here == info_own[1:2, :])
        pick = jnp.where(pick, 1.0, 0.0).astype(jnp.bfloat16)
        return jnp.dot(pick, low_rank, preferred_element_type=jnp.float32).astype(jnp.bfloat16)

    near_rows[y] = pick_rows(y)
    chip_slots = 2 * slots

    def forward_rows(y_from):
        def to_x(x_step, inner):
            x_to = lax.rem(x + near_order(x_step), x_count)
            rows = pl.ds(pl.multiple_of(x_to * chip_slots, chip_slots), chip_slots)
            remote(
                near_rows.at[y_from, rows, :],
                slot_rows.at[x, y_from],
                sent.at[5],
                slot_sem,
                {"dp": x_to},
            ).start()
            return inner

        lax.fori_loop(1, x_count, to_x, 0)
        own = pl.ds(pl.multiple_of(x * chip_slots, chip_slots), chip_slots)
        pltpu.make_async_copy(near_rows.at[y_from, own, :], slot_rows.at[x, y_from], slot_sem).start()

    forward_rows(y)
    for step in range(1, y_count):
        y_to = lax.rem(y + near_order(step), y_count)
        out_rows[step - 1] = pick_rows(y_to)
        remote(
            out_rows.at[step - 1],
            near_rows.at[y],
            sent.at[12],
            near_sem.at[y],
            {"seq": 2 * y_to + c},
        ).start()


    def forward_near(step, carry):
        y_from = lax.rem(y + y_count - near_order(step), y_count)
        wait_bytes(near_rows.at[y_from], near_sem.at[y_from])
        forward_rows(y_from)
        return carry

    lax.fori_loop(1, y_count, forward_near, 0)
    ring_step(down_ring, 3)

    wait_bytes(info_x, info_sem.at[1])
    group = x_count * y_count
    chip_rows = group * slots
    named_all = info_x[...].reshape(group, info_x.shape[2], tok_rows)
    place = lax.broadcasted_iota(jnp.int32, (group, slots, tok_rows), 1)
    weight = []
    for which in range(2):
        slot_here = (place + ((2 * x + which) * y_count + y) * slots).astype(jnp.float32)
        routed = jnp.where(
            slot_here == named_all[:, 0:1, :], named_all[:, 2:3, :], 0.0
        ) + jnp.where(slot_here == named_all[:, 1:2, :], named_all[:, 3:4, :], 0.0)
        weight.append(jnp.sum(routed, axis=2, keepdims=True).reshape(chip_rows, 1))

    wait_bytes(gate_up.at[other_c], pair_g_sem)
    wait_bytes(slot_rows, slot_sem)
    expert = lax.broadcasted_iota(jnp.int32, (chip_rows, 1), 0) % slots // CAP

    for twin_here in range(2):
        rows = slot_rows[:, :, pl.ds(twin_here * slots, slots), :].reshape(chip_rows, rank)
        both_halves = jnp.zeros((chip_rows, gate_up.shape[5]), jnp.float32)
        for which in range(4):
            product = jnp.dot(
                rows,
                gate_up[which // 2, :, twin_here, which % 2].reshape(rank, gate_up.shape[5]),
                preferred_element_type=jnp.float32,
            )
            both_halves = jnp.where(expert == which, product, both_halves)
        gate, up = both_halves[:, :LANES], both_halves[:, LANES:]
        hidden = gate / (1.0 + jnp.exp(-gate)) * up * weight[twin_here]
        hidden_all[x, y, twin_here] = hidden.astype(jnp.bfloat16)
        held = hidden_all.at[x, y, twin_here]

        def hidden_near(step, carry):
            if twin_here == 0:
                device = {"dp": lax.rem(x + near_order(step), x_count)}
            else:
                device = {"seq": 2 * lax.rem(y + near_order(step), y_count) + c}
            remote(held, held, sent.at[15], hid_sem.at[twin_here], device).start()
            return carry

        lax.fori_loop(1, x_count, hidden_near, 0)

    wait_bytes(hidden_all.at[pl.ds(0, x_count - 1), y, 0], hid_sem.at[0])

    def hidden_to_y(step, carry):
        held = hidden_all.at[:, y, 0]
        y_to = lax.rem(y + near_order(step), y_count)
        remote(held, held, sent.at[16], hid_y_sem.at[y], {"seq": 2 * y_to + c}).start()
        return carry

    lax.fori_loop(1, y_count, hidden_to_y, 0)
    wait_bytes(hidden_all.at[x, pl.ds(0, y_count - 1), 1], hid_sem.at[1])

    def hidden_to_x(step, carry):
        held = hidden_all.at[x, :, 1]
        x_to = lax.rem(x + near_order(step), x_count)
        remote(held, held, sent.at[18], hid_x_sem.at[x], {"dp": x_to}).start()
        return carry

    lax.fori_loop(1, x_count, hidden_to_x, 0)
    lax.fori_loop(0, s_count, send_attended, 0)
    ring_step(down_ring, half)
    wait_bytes(weights.at[other_c], pair_w_sem)

    chip_expert = lax.broadcasted_iota(jnp.int32, (chip_rows, LANES), 0) % slots // CAP

    def down_block(x_from, y_from, twin_here):
        held = hidden_all[x_from, y_from, twin_here].astype(jnp.float32)
        z_from = 2 * x_from + twin_here
        masked = [
            jnp.where(chip_expert == which, held, 0.0).astype(jnp.bfloat16) for which in range(4)
        ]
        product = jnp.dot(
            jnp.concatenate(masked[:2], axis=1),
            weights[0, z_from, y_from],
            preferred_element_type=jnp.float32,
        ) + jnp.dot(
            jnp.concatenate(masked[2:], axis=1),
            weights[1, z_from, y_from],
            preferred_element_type=jnp.float32,
        )
        to = pl.ds(pl.multiple_of((z_from * y_count + y_from) * slots, slots), slots)
        slot_out[:, to, :] = product.astype(jnp.bfloat16).reshape(group, slots, cols)

    def down_step(step, carry):
        y_from = lax.rem(y + y_count - near_order(step), y_count)
        x_from = lax.rem(x + x_count - near_order(step), x_count)

        @pl.when(step > 0)
        def _arrive_y():
            wait_bytes(hidden_all.at[:, y_from, 0], hid_y_sem.at[y_from])

        def down_first(other, inner):
            down_block(other, y_from, 0)
            return inner

        lax.fori_loop(0, x_count, down_first, 0)

        @pl.when(step > 0)
        def _arrive_x():
            wait_bytes(hidden_all.at[x_from, :, 1], hid_x_sem.at[x_from])

        def down_second(other, inner):
            down_block(x_from, other, 1)
            return inner

        lax.fori_loop(0, y_count, down_second, 0)
        return carry

    lax.fori_loop(0, y_count, down_step, 0)

    mine = x * y_count + y

    def mix_one(step, carry):
        x_to = lax.rem(x + (step + 1) // y_count, x_count)
        y_to = lax.rem(y + step + 1, y_count)
        to = x_to * y_count + y_to
        slot_iota = lax.broadcasted_iota(jnp.int32, (slot_out.shape[1], tok_rows), 0).astype(
            jnp.float32
        )
        named_here = info_x[x_to, y_to]
        pick = (slot_iota == named_here[0:1, :]) | (slot_iota == named_here[1:2, :])
        pick = jnp.where(pick, 1.0, 0.0).astype(jnp.bfloat16)
        mixed = lax.dot_general(
            pick, slot_out[to], (((0,), (0,)), ((), ())), preferred_element_type=jnp.float32
        )
        mix_out[to] = mixed.astype(jnp.bfloat16)

        @pl.when(to == mine)
        def _keep():
            pltpu.make_async_copy(mix_out.at[to], mix_in.at[mine], mix_sem).start()

        @pl.when(to != mine)
        def _send():
            remote(
                mix_out.at[to],
                mix_in.at[mine],
                sent.at[17],
                mix_sem,
                {"dp": x_to, "seq": 2 * y_to + c},
            ).start()

        return carry

    lax.fori_loop(0, group, mix_one, 0)

    wait_bytes(stream_own, own_sem)
    wait_bytes(attended, att_sem)
    wait_bytes(mix_in, mix_sem)
    for block in range(s_count):
        part = slice(block * head_cols, (block + 1) * head_cols)
        mixed = jnp.concatenate([mix_in[2 * block], mix_in[2 * block + 1, :, LANES:]], axis=1)
        residual = stream_own[:, part].astype(jnp.float32) + attn_gate_ref[:, part].astype(
            jnp.float32
        ) * attended[:, part].astype(jnp.float32)
        output_ref[:, part] = (
            residual + ffn_gate_ref[:, part].astype(jnp.float32) * mixed.astype(jnp.float32)
        ).astype(jnp.bfloat16)

    wait_bytes(info_y.at[pl.ds(0, y_count - 1)], sent.at[0])
    wait_bytes(weights.at[0, 0, pl.ds(0, y_count - 1)], sent.at[1])
    batch_left(1, 0)
    batch_left(1, 1)

    @pl.when(z // 2 == x)
    def _spread_done():
        wait_bytes(gate_up.at[0, pl.ds(0, z_count - 1), 0], sent.at[4])

    wait_bytes(slot_rows.at[pl.ds(0, x_count - 1)], sent.at[5])
    wait_bytes(info_x.at[pl.ds(0, x_count - 1)], sent.at[6])
    wait_bytes(weights.at[0, pl.ds(0, z_count - 1)], sent.at[7])
    wait_bytes(weights.at[0], sent.at[8])
    wait_bytes(core_send, sent.at[9])
    wait_bytes(part_send, sent.at[10])
    wait_bytes(att_out.at[pl.ds(0, s_count - 1)], sent.at[11])
    wait_bytes(out_rows, sent.at[12])
    wait_bytes(gate_up.at[0, pl.ds(0, z_count - 1)], sent.at[13])
    wait_bytes(gate_up.at[0], sent.at[14])
    wait_bytes(hidden_all.at[pl.ds(0, 2), pl.ds(0, y_count - 1), 0], sent.at[15])
    wait_bytes(hidden_all.at[:, pl.ds(0, y_count - 1), 0], sent.at[16])
    wait_bytes(hidden_all.at[pl.ds(0, x_count - 1), :, 1], sent.at[18])
    wait_bytes(mix_out.at[pl.ds(0, group - 1)], sent.at[17])


def on_device(
    query_rows,
    key_rows,
    value_rows,
    stream,
    shared_basis,
    expert_gate_up,
    expert_down,
    attn_gate,
    ffn_scale,
    ffn_gate,
    expert_ids,
    route_weights,
):
    x_count, z_count, s_count = (lax.axis_size(name) for name in ("dp", "exp", "seq"))
    y_count = s_count // 2
    tok_rows, model_width = stream.shape
    experts_here, hidden_cols, _ = expert_down.shape
    expert_total = z_count * s_count * experts_here
    rank = shared_basis.shape[1]
    head_cols = model_width // s_count
    cols = 384
    slots = 4 * CAP
    length = s_count * tok_rows
    group = x_count * y_count

    vmem = pl.BlockSpec(memory_space=pltpu.VMEM)
    anywhere = pl.BlockSpec(memory_space=pl.ANY)
    bf16, f32 = jnp.bfloat16, jnp.float32
    wide = rank + LANES
    dma = pltpu.SemaphoreType.DMA
    return pl.pallas_call(
        block_kernel,
        out_shape=jax.ShapeDtypeStruct((tok_rows, model_width), bf16),
        in_specs=[anywhere] * 6 + [vmem] * 6,
        out_specs=vmem,
        scratch_shapes=[
            pltpu.VMEM((2, length, head_cols), bf16),
            pltpu.VMEM((s_count, 2, tok_rows, head_cols), bf16),
            pltpu.VMEM((tok_rows, model_width), bf16),
            pltpu.VMEM((s_count, tok_rows, head_cols), bf16),
            pltpu.VMEM((tok_rows, model_width), bf16),
            pltpu.VMEM((2 * tok_rows, head_cols), bf16),
            pltpu.VMEM((2, tok_rows, wide), f32),
            pltpu.VMEM((y_count, tok_rows, wide), f32),
            pltpu.VMEM((y_count, tok_rows, wide), bf16),
            pltpu.VMEM((y_count, tok_rows, wide), bf16),
            pltpu.VMEM((y_count - 1, tok_rows, wide), bf16),
            pltpu.VMEM((y_count - 1, tok_rows, wide), bf16),
            pltpu.VMEM((y_count - 1, z_count * slots, rank), bf16),
            pltpu.VMEM((y_count, z_count * slots, rank), bf16),
            pltpu.VMEM((x_count, y_count, 2 * slots, rank), bf16),
            pltpu.VMEM(
                (2, z_count, 2, experts_here, rank // z_count, 2 * hidden_cols), bf16
            ),
            pltpu.VMEM((x_count, y_count, 2, group * slots, hidden_cols), bf16),
            pltpu.VMEM((2, z_count, y_count, experts_here * hidden_cols, cols), bf16),
            pltpu.VMEM((group, z_count * y_count * slots, cols), bf16),
            pltpu.VMEM((group, tok_rows, cols), bf16),
            pltpu.VMEM((group, tok_rows, cols), bf16),
            pltpu.VMEM((8, tok_rows), f32),
            pltpu.VMEM((y_count, 8, tok_rows), f32),
            pltpu.VMEM((x_count, y_count, 8, tok_rows), f32),
            dma,
            dma((s_count,)),
            dma((2, 2)),
            dma,
            dma((2,)),
            dma,
            dma((z_count,)),
            dma,
            dma,
            dma((z_count,)),
            dma,
            dma((y_count,)),
            dma,
            dma,
            dma((y_count,)),
            dma,
            dma((2,)),
            dma((y_count,)),
            dma((x_count,)),
            dma,
            dma((19,)),
        ],
        compiler_params=pltpu.CompilerParams(
            collective_id=0, has_side_effects=True, vmem_limit_bytes=62 * 1024 * 1024
        ),
        name="block",
    )(
        query_rows,
        key_rows,
        value_rows,
        stream,
        expert_down,
        expert_gate_up,
        shared_basis,
        attn_gate,
        ffn_scale,
        ffn_gate,
        expert_ids.T,
        route_weights.T,
    )


def solution(mesh):
    in_specs = (
        P(("dp", "exp", "seq"), None),
        P(("dp", "exp", "seq"), None),
        P(("dp", "exp", "seq"), None),
        P(("dp", "exp", "seq"), None),
        P("seq", None),
        P(("exp", "seq"), None, None),
        P(("exp", "seq"), None, None),
        P(("dp", "exp"), None),
        P(("dp", "exp"), None),
        P(("dp", "exp"), None),
        P(("dp", "exp", "seq"), None),
        P(("dp", "exp", "seq"), None),
    )
    out_specs = P(("dp", "exp", "seq"), None)
    return jax.shard_map(
        on_device, mesh=mesh, in_specs=in_specs, out_specs=out_specs, check_vma=False
    )
```

time: 202 us -> 187 us (0.926)
  the two profiles are of different devices: /device:TPU:64 before, /device:TPU:156 now
where the time goes in v1:
time: 187 us
  Pallas kernels  184 us (98%)
  local copies, waits for them, and re-layouts  2.46 us (1%)
    pallas_call x1, Pallas kernels, on_device(): pl.pallas_call(block_kernel, out_shape=jax.ShapeDtypeStruct((tok_rows, mo...  184 us

profile of v1, /device:TPU:156, one launch (start us, length us, event | category | flops | bytes accessed | tf_op | source)
XLA Modules:
  0.0 186.6 jit_solution(15875507318917407040)
XLA Ops:
  0.0 184.1 %block.1 = bf16[128,5120]{1,0:T(8,128)(2,1)} custom-call(bf16[128,5120]{1,0:T(8,128)(2,1)} %query_ref.1, bf16[128,5120]{1,0:T(8,128)(2,1)} %key_ref.1, bf16[128,5120]{1,0:T(8,128)(2,1)} %value_ref.1, bf16[128,5120]{1,0:T(8,128)(2,1)} %stream_ref.1, bf16[2,128,5120]{2,1,0:T(8,128)(2,1)} %down_ref.1, bf16[2,1024,256]{2,1,0:T(8,128)(2,1)} %gate_up_ref.1, ...), custom_call_target="tpu_custom_call" | custom-call | tf_op jit(solution)/shard_map/block/pallas_call | solution.py:724
  184.1 2.5 %copy.14 = bf16[128,5120]{1,0:T(8,128)(2,1)} copy(bf16[128,5120]{1,0:T(8,128)(2,1)} %block.1) | data formatting | bytes 2621440

commit v2 on v1

--- a/solution.py
+++ b/solution.py
@@ -53,6 +53,8 @@
     info_own,
     info_y,
     info_x,
+    slot_weight,
+    picks,
     kv_sem,
     qs_sem,
     batch_sem,
@@ -167,86 +169,6 @@
             gate_up_ref.at[:, part, :], gate_up.at[c, z, twin], near_g_sem
         ).start()
 
-    pl.semaphore_wait(barrier, s_count - 1 + z_count - 1 + (x_count - 1) * y_count)
-
-    def near_first(step, carry):
-        y_to = lax.rem(y + near_order(step), y_count)
-        device = {"seq": 2 * y_to + c}
-        for which in range(2):
-            remote(
-                down_ref.at[which, :, pl.ds(first_column(y_to), cols)],
-                weights.at[c, z, y, pl.ds(which * LANES, LANES), :],
-                sent.at[1],
-                near_w_sem,
-                device,
-            ).start()
-        return carry
-
-    lax.fori_loop(1, y_count, near_first, 0)
-
-    @pl.when(z // 2 == x)
-    def _spread_gate_up():
-        def to_z(step, carry):
-            z_to = lax.rem(z + step, z_count)
-            part = pl.ds(pl.multiple_of(z_to * rank_part, rank_part), rank_part)
-            remote(
-                gate_up_ref.at[:, part, :],
-                gate_up.at[c, z_to, twin],
-                sent.at[4],
-                near_g_sem,
-                {"exp": z_to},
-            ).start()
-            return carry
-
-        lax.fori_loop(1, z_count, to_z, 0)
-
-
-    def send_batch(refs, slot_of, sem, send_sem, distances):
-        def one_copy(index, carry):
-            s_to = 2 * lax.rem(y + distances[0] + 2 * (index % len(distances)), y_count) + (
-                index // len(distances)
-            )
-            columns = pl.ds(pl.multiple_of(s_to * head_cols, head_cols), head_cols)
-            for which in range(2):
-                remote(
-                    refs[which].at[:, columns], slot_of(which), send_sem, sem, {"seq": s_to}
-                ).start()
-            return carry
-
-        if len(distances) == 2:
-            columns = pl.ds(pl.multiple_of(pair * head_cols, head_cols), head_cols)
-            for which in range(2):
-                remote(
-                    refs[which].at[:, columns], slot_of(which), send_sem, sem, {"seq": pair}
-                ).start()
-        lax.fori_loop(0, 2 * len(distances), one_copy, 0)
-
-    batches = ((1, 3), (2,))
-
-    def send_kv(batch):
-        send_batch(
-            kv_refs,
-            lambda which: kv_in.at[which, my_rows, :],
-            kv_sem,
-            batch_sem.at[0, batch],
-            batches[batch],
-        )
-
-    def send_qs(batch):
-        send_batch(
-            qs_refs,
-            lambda which: qs_in.at[s, which],
-            qs_sem.at[s],
-            batch_sem.at[1, batch],
-            batches[batch],
-        )
-
-    def batch_left(kind, batch):
-        peers = 5 if batch == 0 else 2
-        wait_bytes(qs_in.at[pl.ds(0, peers)], batch_sem.at[kind, batch])
-
-    send_kv(0)
-
     entries = 2 * tok_rows
     experts = 4 * z_count * y_count
     ids_row = jnp.concatenate([ids_ref[0:1, :], ids_ref[1:2, :]], axis=1)
@@ -268,6 +190,8 @@
     info_own[...] = jnp.where(info_row == 1, slot_ids[:, tok_rows:], info)
     pltpu.make_async_copy(info_own, info_y.at[y], info_sem.at[0]).start()
 
+    pl.semaphore_wait(barrier, s_count - 1 + z_count - 1 + (x_count - 1) * y_count)
+
     def info_to_y(step, carry):
         y_to = lax.rem(y + step, y_count)
         remote(
@@ -276,6 +200,84 @@
         return carry
 
     lax.fori_loop(1, y_count, info_to_y, 0)
+
+    def near_first(step, carry):
+        y_to = lax.rem(y + near_order(step), y_count)
+        device = {"seq": 2 * y_to + c}
+        for which in range(2):
+            remote(
+                down_ref.at[which, :, pl.ds(first_column(y_to), cols)],
+                weights.at[c, z, y, pl.ds(which * LANES, LANES), :],
+                sent.at[1],
+                near_w_sem,
+                device,
+            ).start()
+        return carry
+
+    lax.fori_loop(1, y_count, near_first, 0)
+
+    @pl.when(z // 2 == x)
+    def _spread_gate_up():
+        def to_z(step, carry):
+            z_to = lax.rem(z + step, z_count)
+            part = pl.ds(pl.multiple_of(z_to * rank_part, rank_part), rank_part)
+            remote(
+                gate_up_ref.at[:, part, :],
+                gate_up.at[c, z_to, twin],
+                sent.at[4],
+                near_g_sem,
+                {"exp": z_to},
+            ).start()
+            return carry
+
+        lax.fori_loop(1, z_count, to_z, 0)
+
+
+    def send_batch(refs, slot_of, sem, send_sem, distances):
+        def one_copy(index, carry):
+            s_to = 2 * lax.rem(y + distances[0] + 2 * (index % len(distances)), y_count) + (
+                index // len(distances)
+            )
+            columns = pl.ds(pl.multiple_of(s_to * head_cols, head_cols), head_cols)
+            for which in range(2):
+                remote(
+                    refs[which].at[:, columns], slot_of(which), send_sem, sem, {"seq": s_to}
+                ).start()
+            return carry
+
+        if len(distances) == 2:
+            columns = pl.ds(pl.multiple_of(pair * head_cols, head_cols), head_cols)
+            for which in range(2):
+                remote(
+                    refs[which].at[:, columns], slot_of(which), send_sem, sem, {"seq": pair}
+                ).start()
+        lax.fori_loop(0, 2 * len(distances), one_copy, 0)
+
+    batches = ((1, 3), (2,))
+
+    def send_kv(batch):
+        send_batch(
+            kv_refs,
+            lambda which: kv_in.at[which, my_rows, :],
+            kv_sem,
+            batch_sem.at[0, batch],
+            batches[batch],
+        )
+
+    def send_qs(batch):
+        send_batch(
+            qs_refs,
+            lambda which: qs_in.at[s, which],
+            qs_sem.at[s],
+            batch_sem.at[1, batch],
+            batches[batch],
+        )
+
+    def batch_left(kind, batch):
+        peers = 5 if batch == 0 else 2
+        wait_bytes(qs_in.at[pl.ds(0, peers)], batch_sem.at[kind, batch])
+
+    send_kv(0)
 
     always = z >= 0
     half = z_count // 2
@@ -316,6 +318,20 @@
     down_ring = (weights, ring_sem, sent.at[7], sent.at[8], pair_w_sem)
 
     wait_bytes(gate_up.at[c, z], near_g_sem)
+    wait_bytes(info_y, info_sem.at[0])
+    pltpu.make_async_copy(info_y, info_x.at[x], info_sem.at[1]).start()
+
+    def info_to_x(step, carry):
+        remote(
+            info_y,
+            info_x.at[x],
+            sent.at[6],
+            info_sem.at[1],
+            {"dp": lax.rem(x + step, x_count)},
+        ).start()
+        return carry
+
+    lax.fori_loop(1, x_count, info_to_x, 0)
     pass_on(*gate_ring, z, always, always)
     send_kv(1)
     ring_step(gate_ring, 1)
@@ -326,20 +342,28 @@
     ring_step(gate_ring, 2)
     ring_step(gate_ring, 3)
 
-    wait_bytes(info_y, info_sem.at[0])
-    pltpu.make_async_copy(info_y, info_x.at[x], info_sem.at[1]).start()
-
-    def info_to_x(step, carry):
-        remote(
-            info_y,
-            info_x.at[x],
-            sent.at[6],
-            info_sem.at[1],
-            {"dp": lax.rem(x + step, x_count)},
-        ).start()
-        return carry
-
-    lax.fori_loop(1, x_count, info_to_x, 0)
+    wait_bytes(info_x, info_sem.at[1])
+    group = x_count * y_count
+    chip_rows = group * slots
+    named_all = info_x[...].reshape(group, info_x.shape[2], tok_rows)
+    place = lax.broadcasted_iota(jnp.int32, (group, slots, tok_rows), 1)
+    for which in range(2):
+        slot_here = (place + ((2 * x + which) * y_count + y) * slots).astype(jnp.float32)
+        routed = jnp.where(
+            slot_here == named_all[:, 0:1, :], named_all[:, 2:3, :], 0.0
+        ) + jnp.where(slot_here == named_all[:, 1:2, :], named_all[:, 3:4, :], 0.0)
+        slot_weight[which] = jnp.sum(routed, axis=2, keepdims=True).reshape(chip_rows, 1)
+
+    def make_pick(source, carry):
+        slot_iota = lax.broadcasted_iota(jnp.int32, (picks.shape[2], tok_rows), 0).astype(
+            jnp.float32
+        )
+        named_here = info_x[source // y_count, source % y_count]
+        pick = (slot_iota == named_here[0:1, :]) | (slot_iota == named_here[1:2, :])
+        picks[source] = jnp.where(pick, 1.0, 0.0).T.astype(jnp.bfloat16)
+        return carry
+
+    lax.fori_loop(0, group, make_pick, 0)
     wait_bytes(kv_in, kv_sem)
 
     length = s_count * tok_rows
@@ -423,13 +447,9 @@
             batch_left(0, 1)
             send_qs(1)
 
-        @pl.when(step == 1)
+        @pl.when(step == 2)
         def _ring_one():
             ring_step(down_ring, 1)
-
-        @pl.when(step == 2)
-        def _ring_two():
-            ring_step(down_ring, 2)
 
         return carry
 
@@ -464,7 +484,6 @@
         pick = jnp.where(pick, 1.0, 0.0).astype(jnp.bfloat16)
         return jnp.dot(pick, low_rank, preferred_element_type=jnp.float32).astype(jnp.bfloat16)
 
-    near_rows[y] = pick_rows(y)
     chip_slots = 2 * slots
 
     def forward_rows(y_from):
@@ -484,7 +503,6 @@
         own = pl.ds(pl.multiple_of(x * chip_slots, chip_slots), chip_slots)
         pltpu.make_async_copy(near_rows.at[y_from, own, :], slot_rows.at[x, y_from], slot_sem).start()
 
-    forward_rows(y)
     for step in range(1, y_count):
         y_to = lax.rem(y + near_order(step), y_count)
         out_rows[step - 1] = pick_rows(y_to)
@@ -497,6 +515,10 @@
         ).start()
 
 
+    near_rows[y] = pick_rows(y)
+    forward_rows(y)
+    ring_step(down_ring, 2)
+
     def forward_near(step, carry):
         y_from = lax.rem(y + y_count - near_order(step), y_count)
         wait_bytes(near_rows.at[y_from], near_sem.at[y_from])
@@ -504,20 +526,6 @@
         return carry
 
     lax.fori_loop(1, y_count, forward_near, 0)
-    ring_step(down_ring, 3)
-
-    wait_bytes(info_x, info_sem.at[1])
-    group = x_count * y_count
-    chip_rows = group * slots
-    named_all = info_x[...].reshape(group, info_x.shape[2], tok_rows)
-    place = lax.broadcasted_iota(jnp.int32, (group, slots, tok_rows), 1)
-    weight = []
-    for which in range(2):
-        slot_here = (place + ((2 * x + which) * y_count + y) * slots).astype(jnp.float32)
-        routed = jnp.where(
-            slot_here == named_all[:, 0:1, :], named_all[:, 2:3, :], 0.0
-        ) + jnp.where(slot_here == named_all[:, 1:2, :], named_all[:, 3:4, :], 0.0)
-        weight.append(jnp.sum(routed, axis=2, keepdims=True).reshape(chip_rows, 1))
 
     wait_bytes(gate_up.at[other_c], pair_g_sem)
     wait_bytes(slot_rows, slot_sem)
@@ -534,7 +542,7 @@
             )
             both_halves = jnp.where(expert == which, product, both_halves)
         gate, up = both_halves[:, :LANES], both_halves[:, LANES:]
-        hidden = gate / (1.0 + jnp.exp(-gate)) * up * weight[twin_here]
+        hidden = gate / (1.0 + jnp.exp(-gate)) * up * slot_weight[twin_here]
         hidden_all[x, y, twin_here] = hidden.astype(jnp.bfloat16)
         held = hidden_all.at[x, y, twin_here]
 
@@ -548,6 +556,7 @@
 
         lax.fori_loop(1, x_count, hidden_near, 0)
 
+    ring_step(down_ring, 3)
     wait_bytes(hidden_all.at[pl.ds(0, x_count - 1), y, 0], hid_sem.at[0])
 
     def hidden_to_y(step, carry):
@@ -572,12 +581,14 @@
 
     chip_expert = lax.broadcasted_iota(jnp.int32, (chip_rows, LANES), 0) % slots // CAP
 
+    masks = [
+        jnp.where(chip_expert == which, 1.0, 0.0).astype(jnp.bfloat16) for which in range(4)
+    ]
+
     def down_block(x_from, y_from, twin_here):
-        held = hidden_all[x_from, y_from, twin_here].astype(jnp.float32)
+        held = hidden_all[x_from, y_from, twin_here]
         z_from = 2 * x_from + twin_here
-        masked = [
-            jnp.where(chip_expert == which, held, 0.0).astype(jnp.bfloat16) for which in range(4)
-        ]
+        masked = [held * mask for mask in masks]
         product = jnp.dot(
             jnp.concatenate(masked[:2], axis=1),
             weights[0, z_from, y_from],
@@ -623,20 +634,12 @@
         x_to = lax.rem(x + (step + 1) // y_count, x_count)
         y_to = lax.rem(y + step + 1, y_count)
         to = x_to * y_count + y_to
-        slot_iota = lax.broadcasted_iota(jnp.int32, (slot_out.shape[1], tok_rows), 0).astype(
-            jnp.float32
-        )
-        named_here = info_x[x_to, y_to]
-        pick = (slot_iota == named_here[0:1, :]) | (slot_iota == named_here[1:2, :])
-        pick = jnp.where(pick, 1.0, 0.0).astype(jnp.bfloat16)
-        mixed = lax.dot_general(
-            pick, slot_out[to], (((0,), (0,)), ((), ())), preferred_element_type=jnp.float32
-        )
+        mixed = jnp.dot(picks[to], slot_out[to], preferred_element_type=jnp.float32)
         mix_out[to] = mixed.astype(jnp.bfloat16)
 
         @pl.when(to == mine)
         def _keep():
-            pltpu.make_async_copy(mix_out.at[to], mix_in.at[mine], mix_sem).start()
+            pltpu.make_async_copy(mix_out.at[to], mix_in.at[mine], mix_sem.at[mine]).start()
 
         @pl.when(to != mine)
         def _send():
@@ -644,7 +647,7 @@
                 mix_out.at[to],
                 mix_in.at[mine],
                 sent.at[17],
-                mix_sem,
+                mix_sem.at[mine],
                 {"dp": x_to, "seq": 2 * y_to + c},
             ).start()
 
@@ -654,9 +657,10 @@
 
     wait_bytes(stream_own, own_sem)
     wait_bytes(attended, att_sem)
-    wait_bytes(mix_in, mix_sem)
     for block in range(s_count):
         part = slice(block * head_cols, (block + 1) * head_cols)
+        for part_of in (2 * block, 2 * block + 1):
+            wait_bytes(mix_in.at[part_of], mix_sem.at[part_of])
         mixed = jnp.concatenate([mix_in[2 * block], mix_in[2 * block + 1, :, LANES:]], axis=1)
         residual = stream_own[:, part].astype(jnp.float32) + attn_gate_ref[:, part].astype(
             jnp.float32
@@ -753,6 +757,8 @@
             pltpu.VMEM((8, tok_rows), f32),
             pltpu.VMEM((y_count, 8, tok_rows), f32),
             pltpu.VMEM((x_count, y_count, 8, tok_rows), f32),
+            pltpu.VMEM((2, group * slots, 1), f32),
+            pltpu.VMEM((group, tok_rows, group * 2 * slots), bf16),
             dma,
             dma((s_count,)),
             dma((2, 2)),
@@ -772,7 +778,7 @@
             dma((2,)),
             dma((y_count,)),
             dma((x_count,)),
-            dma,
+            dma((group,)),
             dma((19,)),
         ],
         compiler_params=pltpu.CompilerParams(

time: 187 us -> 173 us (0.925)
  the two profiles are of different devices: /device:TPU:156 before, /device:TPU:1 now
where the time goes in v2:
time: 173 us; the launch traced here: 172 us
  Pallas kernels  170 us (98%)
  local copies, waits for them, and re-layouts  2.46 us (1%)
    pallas_call x1, Pallas kernels, on_device(): pl.pallas_call(block_kernel, out_shape=jax.ShapeDtypeStruct((tok_rows, mo...  170 us

profile of v2, /device:TPU:1, one launch (start us, length us, event | category | flops | bytes accessed | tf_op | source)
XLA Modules:
  0.0 172.1 jit_solution(5465753962770160675)
XLA Ops:
  0.0 169.6 %block.1 = bf16[128,5120]{1,0:T(8,128)(2,1)} custom-call(bf16[128,5120]{1,0:T(8,128)(2,1)} %query_ref.1, bf16[128,5120]{1,0:T(8,128)(2,1)} %key_ref.1, bf16[128,5120]{1,0:T(8,128)(2,1)} %value_ref.1, bf16[128,5120]{1,0:T(8,128)(2,1)} %stream_ref.1, bf16[2,128,5120]{2,1,0:T(8,128)(2,1)} %down_ref.1, bf16[2,1024,256]{2,1,0:T(8,128)(2,1)} %gate_up_ref.1, ...), custom_call_target="tpu_custom_call" | custom-call | tf_op jit(solution)/shard_map/block/pallas_call | solution.py:728
  169.7 2.5 %copy.14 = bf16[128,5120]{1,0:T(8,128)(2,1)} copy(bf16[128,5120]{1,0:T(8,128)(2,1)} %block.1) | data formatting | bytes 2621440

commit v3 on v2

--- a/solution.py
+++ b/solution.py
@@ -341,6 +341,8 @@
     send_qs(0)
     ring_step(gate_ring, 2)
     ring_step(gate_ring, 3)
+    batch_left(0, 1)
+    send_qs(1)
 
     wait_bytes(info_x, info_sem.at[1])
     group = x_count * y_count
@@ -444,8 +446,6 @@
         @pl.when(step == 0)
         def _last_batch():
             ring_step(gate_ring, half)
-            batch_left(0, 1)
-            send_qs(1)
 
         @pl.when(step == 2)
         def _ring_one():
@@ -456,7 +456,9 @@
     lax.fori_loop(0, y_count, after_chip, 0)
     send_part(y_count - 1)
 
-    def send_attended(s_to, carry):
+    def send_attended(index, carry):
+        s_to = lax.rem(s + index, s_count)
+
         @pl.when(s_to == s)
         def _keep():
             pltpu.make_async_copy(att_out.at[s_to], attended.at[:, my_cols], att_sem).start()
@@ -523,8 +525,9 @@
         y_from = lax.rem(y + y_count - near_order(step), y_count)
         wait_bytes(near_rows.at[y_from], near_sem.at[y_from])
         forward_rows(y_from)
-        return carry
-
+        return lax.fori_loop(2 * step, 2 * step + 2, send_attended, carry)
+
+    lax.fori_loop(0, 2, send_attended, 0)
     lax.fori_loop(1, y_count, forward_near, 0)
 
     wait_bytes(gate_up.at[other_c], pair_g_sem)
@@ -575,7 +578,6 @@
         return carry
 
     lax.fori_loop(1, x_count, hidden_to_x, 0)
-    lax.fori_loop(0, s_count, send_attended, 0)
     ring_step(down_ring, half)
     wait_bytes(weights.at[other_c], pair_w_sem)
 
@@ -637,19 +639,35 @@
         mixed = jnp.dot(picks[to], slot_out[to], preferred_element_type=jnp.float32)
         mix_out[to] = mixed.astype(jnp.bfloat16)
 
-        @pl.when(to == mine)
-        def _keep():
-            pltpu.make_async_copy(mix_out.at[to], mix_in.at[mine], mix_sem.at[mine]).start()
-
-        @pl.when(to != mine)
-        def _send():
-            remote(
-                mix_out.at[to],
-                mix_in.at[mine],
-                sent.at[17],
-                mix_sem.at[mine],
-                {"dp": x_to, "seq": 2 * y_to + c},
-            ).start()
+        def give(first, last):
+            source = mix_out.at[to, :, first:last]
+            target = mix_in.at[mine, :, first:last]
+
+            @pl.when(to == mine)
+            def _keep():
+                pltpu.make_async_copy(source, target, mix_sem.at[mine]).start()
+
+            @pl.when(to != mine)
+            def _send():
+                remote(
+                    source,
+                    target,
+                    sent.at[17],
+                    mix_sem.at[mine],
+                    {"dp": x_to, "seq": 2 * y_to + c},
+                ).start()
+
+        @pl.when(y % 2 == c)
+        def _whole():
+            give(0, cols)
+
+        @pl.when((y % 2 == 0) & (c == 1))
+        def _low():
+            give(0, cols - LANES)
+
+        @pl.when((y % 2 == 1) & (c == 0))
+        def _high():
+            give(LANES, cols)
 
         return carry
 
@@ -657,17 +675,32 @@
 
     wait_bytes(stream_own, own_sem)
     wait_bytes(attended, att_sem)
-    for block in range(s_count):
-        part = slice(block * head_cols, (block + 1) * head_cols)
-        for part_of in (2 * block, 2 * block + 1):
-            wait_bytes(mix_in.at[part_of], mix_sem.at[part_of])
-        mixed = jnp.concatenate([mix_in[2 * block], mix_in[2 * block + 1, :, LANES:]], axis=1)
-        residual = stream_own[:, part].astype(jnp.float32) + attn_gate_ref[:, part].astype(
-            jnp.float32
-        ) * attended[:, part].astype(jnp.float32)
-        output_ref[:, part] = (
-            residual + ffn_gate_ref[:, part].astype(jnp.float32) * mixed.astype(jnp.float32)
-        ).astype(jnp.bfloat16)
+
+    def finish(core):
+        for block in range(s_count):
+            part = slice(block * head_cols, (block + 1) * head_cols)
+            even, odd = 2 * block, 2 * block + 1
+            if core == 0:
+                wait_bytes(mix_in.at[even], mix_sem.at[even])
+                wait_bytes(mix_in.at[odd, :, LANES:cols], mix_sem.at[odd])
+                mixed = [mix_in[even], mix_in[odd, :, LANES:]]
+            else:
+                wait_bytes(mix_in.at[even, :, 0 : cols - LANES], mix_sem.at[even])
+                wait_bytes(mix_in.at[odd], mix_sem.at[odd])
+                mixed = [mix_in[even, :, : cols - LANES], mix_in[odd]]
+            mixed = jnp.concatenate(mixed, axis=1)
+            residual = stream_own[:, part].astype(jnp.float32) + attn_gate_ref[:, part].astype(
+                jnp.float32
+            ) * attended[:, part].astype(jnp.float32)
+            output_ref[:, part] = (
+                residual + ffn_gate_ref[:, part].astype(jnp.float32) * mixed.astype(jnp.float32)
+            ).astype(jnp.bfloat16)
+
+    for core in range(2):
+
+        @pl.when(c == core)
+        def _finish():
+            finish(core)
 
     wait_bytes(info_y.at[pl.ds(0, y_count - 1)], sent.at[0])
     wait_bytes(weights.at[0, 0, pl.ds(0, y_count - 1)], sent.at[1])
@@ -691,7 +724,14 @@
     wait_bytes(hidden_all.at[pl.ds(0, 2), pl.ds(0, y_count - 1), 0], sent.at[15])
     wait_bytes(hidden_all.at[:, pl.ds(0, y_count - 1), 0], sent.at[16])
     wait_bytes(hidden_all.at[pl.ds(0, x_count - 1), :, 1], sent.at[18])
-    wait_bytes(mix_out.at[pl.ds(0, group - 1)], sent.at[17])
+
+    @pl.when(y % 2 == c)
+    def _whole_done():
+        wait_bytes(mix_out.at[pl.ds(0, group - 1)], sent.at[17])
+
+    @pl.when(y % 2 != c)
+    def _part_done():
+        wait_bytes(mix_out.at[pl.ds(0, group - 1), :, 0 : cols - LANES], sent.at[17])
 
 
 def on_device(

time: 173 us -> 168 us (0.971)
  Pallas kernels: 170 us -> 165 us
    pallas_call x1, Pallas kernels: 170 us -> 165 us  [on_device(): pl.pallas_call(block_kernel, out_shape=jax.ShapeDtypeStruct((tok_rows, mo...]
where the time goes in v3:
time: 168 us
  Pallas kernels  165 us (98%)
  local copies, waits for them, and re-layouts  2.46 us (1%)
    pallas_call x1, Pallas kernels, on_device(): pl.pallas_call(block_kernel, out_shape=jax.ShapeDtypeStruct((tok_rows, mo...  165 us

profile of v3, /device:TPU:1, one launch (start us, length us, event | category | flops | bytes accessed | tf_op | source)
XLA Modules:
  0.0 167.8 jit_solution(9797090483406761127)
XLA Ops:
  0.0 165.4 %block.1 = bf16[128,5120]{1,0:T(8,128)(2,1)} custom-call(bf16[128,5120]{1,0:T(8,128)(2,1)} %query_ref.1, bf16[128,5120]{1,0:T(8,128)(2,1)} %key_ref.1, bf16[128,5120]{1,0:T(8,128)(2,1)} %value_ref.1, bf16[128,5120]{1,0:T(8,128)(2,1)} %stream_ref.1, bf16[2,128,5120]{2,1,0:T(8,128)(2,1)} %down_ref.1, bf16[2,1024,256]{2,1,0:T(8,128)(2,1)} %gate_up_ref.1, ...), custom_call_target="tpu_custom_call" | custom-call | tf_op jit(solution)/shard_map/block/pallas_call | solution.py:768
  165.4 2.5 %copy.14 = bf16[128,5120]{1,0:T(8,128)(2,1)} copy(bf16[128,5120]{1,0:T(8,128)(2,1)} %block.1) | data formatting | bytes 2621440

commit v4 on v3

--- a/solution.py
+++ b/solution.py
@@ -347,25 +347,15 @@
     wait_bytes(info_x, info_sem.at[1])
     group = x_count * y_count
     chip_rows = group * slots
-    named_all = info_x[...].reshape(group, info_x.shape[2], tok_rows)
-    place = lax.broadcasted_iota(jnp.int32, (group, slots, tok_rows), 1)
-    for which in range(2):
-        slot_here = (place + ((2 * x + which) * y_count + y) * slots).astype(jnp.float32)
-        routed = jnp.where(
-            slot_here == named_all[:, 0:1, :], named_all[:, 2:3, :], 0.0
-        ) + jnp.where(slot_here == named_all[:, 1:2, :], named_all[:, 3:4, :], 0.0)
-        slot_weight[which] = jnp.sum(routed, axis=2, keepdims=True).reshape(chip_rows, 1)
-
     def make_pick(source, carry):
         slot_iota = lax.broadcasted_iota(jnp.int32, (picks.shape[2], tok_rows), 0).astype(
             jnp.float32
         )
         named_here = info_x[source // y_count, source % y_count]
         pick = (slot_iota == named_here[0:1, :]) | (slot_iota == named_here[1:2, :])
-        picks[source] = jnp.where(pick, 1.0, 0.0).T.astype(jnp.bfloat16)
-        return carry
-
-    lax.fori_loop(0, group, make_pick, 0)
+        picks[source] = jnp.where(pick, 1.0, 0.0).astype(jnp.bfloat16).T
+        return carry
+
     wait_bytes(kv_in, kv_sem)
 
     length = s_count * tok_rows
@@ -523,11 +513,21 @@
 
     def forward_near(step, carry):
         y_from = lax.rem(y + y_count - near_order(step), y_count)
+        lax.fori_loop(4 * step - 4, 4 * step, make_pick, 0)
         wait_bytes(near_rows.at[y_from], near_sem.at[y_from])
         forward_rows(y_from)
         return lax.fori_loop(2 * step, 2 * step + 2, send_attended, carry)
 
     lax.fori_loop(0, 2, send_attended, 0)
+    named_all = info_x[...].reshape(group, info_x.shape[2], tok_rows)
+    place = lax.broadcasted_iota(jnp.int32, (group, slots, tok_rows), 1)
+    for which in range(2):
+        slot_here = (place + ((2 * x + which) * y_count + y) * slots).astype(jnp.float32)
+        routed = jnp.where(
+            slot_here == named_all[:, 0:1, :], named_all[:, 2:3, :], 0.0
+        ) + jnp.where(slot_here == named_all[:, 1:2, :], named_all[:, 3:4, :], 0.0)
+        slot_weight[which] = jnp.sum(routed, axis=2, keepdims=True).reshape(chip_rows, 1)
+
     lax.fori_loop(1, y_count, forward_near, 0)
 
     wait_bytes(gate_up.at[other_c], pair_g_sem)
@@ -560,6 +560,7 @@
         lax.fori_loop(1, x_count, hidden_near, 0)
 
     ring_step(down_ring, 3)
+    lax.fori_loop(4 * (y_count - 1), group, make_pick, 0)
     wait_bytes(hidden_all.at[pl.ds(0, x_count - 1), y, 0], hid_sem.at[0])
 
     def hidden_to_y(step, carry):

time: 168 us -> 168 us (level)
  no operation moved by 1% of the time
where the time goes in v4:
time: 168 us; the launch traced here: 167 us
  Pallas kernels  165 us (98%)
  local copies, waits for them, and re-layouts  2.46 us (1%)
    pallas_call x1, Pallas kernels, on_device(): pl.pallas_call(block_kernel, out_shape=jax.ShapeDtypeStruct((tok_rows, mo...  165 us

profile of v4, /device:TPU:1, one launch (start us, length us, event | category | flops | bytes accessed | tf_op | source)
XLA Modules:
  0.0 167.4 jit_solution(16747392673401899329)
XLA Ops:
  0.0 164.9 %block.1 = bf16[128,5120]{1,0:T(8,128)(2,1)} custom-call(bf16[128,5120]{1,0:T(8,128)(2,1)} %query_ref.1, bf16[128,5120]{1,0:T(8,128)(2,1)} %key_ref.1, bf16[128,5120]{1,0:T(8,128)(2,1)} %value_ref.1, bf16[128,5120]{1,0:T(8,128)(2,1)} %stream_ref.1, bf16[2,128,5120]{2,1,0:T(8,128)(2,1)} %down_ref.1, bf16[2,1024,256]{2,1,0:T(8,128)(2,1)} %gate_up_ref.1, ...), custom_call_target="tpu_custom_call" | custom-call | tf_op jit(solution)/shard_map/block/pallas_call | solution.py:769
  164.9 2.5 %copy.14 = bf16[128,5120]{1,0:T(8,128)(2,1)} copy(bf16[128,5120]{1,0:T(8,128)(2,1)} %block.1) | data formatting | bytes 2621440

commit v5 on v4

--- a/solution.py
+++ b/solution.py
@@ -87,7 +87,7 @@
     head_cols = kv_in.shape[2]
     heads_here = head_cols // HEAD_DIM
     cols = weights.shape[4]
-    rank = near_rows.shape[2]
+    rank = near_rows.shape[3]
     slots = 4 * CAP
     quarter = model_width // x_count
 
@@ -391,6 +391,26 @@
             {"seq": 2 * y_to + c},
         ).start()
 
+    def send_attended(step):
+        y_to = lax.rem(y + y_count - near_order(step), y_count)
+
+        def one_core(core, carry):
+            s_to = 2 * y_to + core
+
+            @pl.when(s_to == s)
+            def _keep():
+                pltpu.make_async_copy(att_out.at[s_to], attended.at[:, my_cols], att_sem).start()
+
+            @pl.when(s_to != s)
+            def _send():
+                remote(
+                    att_out.at[s_to], attended.at[:, my_cols], sent.at[11], att_sem, {"seq": s_to}
+                ).start()
+
+            return carry
+
+        lax.fori_loop(0, 2, one_core, 0)
+
     def one_chip(step, carry):
         y_from = lax.rem(y + y_count - near_order(step), y_count)
 
@@ -400,6 +420,12 @@
 
         for core in range(2):
             wait_bytes(qs_in.at[2 * y_from + core], qs_sem.at[2 * y_from + core])
+
+        @pl.when(step == y_count - 1)
+        def _earlier():
+            for earlier in range(y_count - 1):
+                send_attended(earlier)
+
         both = pl.ds(2 * y_from, 2)
         square = jnp.zeros((two, 1), jnp.float32)
         for head in range(heads_here):
@@ -446,21 +472,6 @@
     lax.fori_loop(0, y_count, after_chip, 0)
     send_part(y_count - 1)
 
-    def send_attended(index, carry):
-        s_to = lax.rem(s + index, s_count)
-
-        @pl.when(s_to == s)
-        def _keep():
-            pltpu.make_async_copy(att_out.at[s_to], attended.at[:, my_cols], att_sem).start()
-
-        @pl.when(s_to != s)
-        def _send():
-            remote(
-                att_out.at[s_to], attended.at[:, my_cols], sent.at[11], att_sem, {"seq": s_to}
-            ).start()
-
-        return carry
-
     values, square = add_core_part(0)
     wait_bytes(part_recv, part_sem)
     for step in range(y_count - 1):
@@ -469,56 +480,52 @@
         square = square + arrived[:, rank : rank + 1] + arrived[:, rank + 1 : rank + 2]
     low_rank = (values / jnp.sqrt(square / model_width + epsilon)).astype(jnp.bfloat16)
 
-    def pick_rows(y_to):
-        row = lax.broadcasted_iota(jnp.int32, (z_count * slots, tok_rows), 0)
-        slot_here = (((row // slots) * y_count + y_to) * slots + row % slots).astype(jnp.float32)
+    def pick_rows(y_to, twin_here):
+        row = lax.broadcasted_iota(jnp.int32, (x_count * slots, tok_rows), 0)
+        chip = (2 * (row // slots) + twin_here) * y_count + y_to
+        slot_here = (chip * slots + row % slots).astype(jnp.float32)
         pick = (slot_here == info_own[0:1, :]) | (slot_here == info_own[1:2, :])
         pick = jnp.where(pick, 1.0, 0.0).astype(jnp.bfloat16)
         return jnp.dot(pick, low_rank, preferred_element_type=jnp.float32).astype(jnp.bfloat16)
 
-    chip_slots = 2 * slots
-
-    def forward_rows(y_from):
+    def forward_rows(y_from, twin_here):
         def to_x(x_step, inner):
             x_to = lax.rem(x + near_order(x_step), x_count)
-            rows = pl.ds(pl.multiple_of(x_to * chip_slots, chip_slots), chip_slots)
+            rows = pl.ds(pl.multiple_of(x_to * slots, slots), slots)
             remote(
-                near_rows.at[y_from, rows, :],
-                slot_rows.at[x, y_from],
+                near_rows.at[twin_here, y_from, rows, :],
+                slot_rows.at[twin_here, x, y_from],
                 sent.at[5],
-                slot_sem,
+                slot_sem.at[twin_here],
                 {"dp": x_to},
             ).start()
             return inner
 
         lax.fori_loop(1, x_count, to_x, 0)
-        own = pl.ds(pl.multiple_of(x * chip_slots, chip_slots), chip_slots)
-        pltpu.make_async_copy(near_rows.at[y_from, own, :], slot_rows.at[x, y_from], slot_sem).start()
-
-    for step in range(1, y_count):
-        y_to = lax.rem(y + near_order(step), y_count)
-        out_rows[step - 1] = pick_rows(y_to)
-        remote(
-            out_rows.at[step - 1],
-            near_rows.at[y],
-            sent.at[12],
-            near_sem.at[y],
-            {"seq": 2 * y_to + c},
+        own = pl.ds(pl.multiple_of(x * slots, slots), slots)
+        pltpu.make_async_copy(
+            near_rows.at[twin_here, y_from, own, :],
+            slot_rows.at[twin_here, x, y_from],
+            slot_sem.at[twin_here],
         ).start()
 
-
-    near_rows[y] = pick_rows(y)
-    forward_rows(y)
+    for twin_here in range(2):
+        for step in range(1, y_count):
+            y_to = lax.rem(y + near_order(step), y_count)
+            out_rows[step - 1, twin_here] = pick_rows(y_to, twin_here)
+            remote(
+                out_rows.at[step - 1, twin_here],
+                near_rows.at[twin_here, y],
+                sent.at[12],
+                near_sem.at[twin_here, y],
+                {"seq": 2 * y_to + c},
+            ).start()
+        near_rows[twin_here, y] = pick_rows(y, twin_here)
+        forward_rows(y, twin_here)
+
     ring_step(down_ring, 2)
-
-    def forward_near(step, carry):
-        y_from = lax.rem(y + y_count - near_order(step), y_count)
-        lax.fori_loop(4 * step - 4, 4 * step, make_pick, 0)
-        wait_bytes(near_rows.at[y_from], near_sem.at[y_from])
-        forward_rows(y_from)
-        return lax.fori_loop(2 * step, 2 * step + 2, send_attended, carry)
-
-    lax.fori_loop(0, 2, send_attended, 0)
+    send_attended(y_count - 1)
+
     named_all = info_x[...].reshape(group, info_x.shape[2], tok_rows)
     place = lax.broadcasted_iota(jnp.int32, (group, slots, tok_rows), 1)
     for which in range(2):
@@ -528,14 +535,24 @@
         ) + jnp.where(slot_here == named_all[:, 1:2, :], named_all[:, 3:4, :], 0.0)
         slot_weight[which] = jnp.sum(routed, axis=2, keepdims=True).reshape(chip_rows, 1)
 
-    lax.fori_loop(1, y_count, forward_near, 0)
-
-    wait_bytes(gate_up.at[other_c], pair_g_sem)
-    wait_bytes(slot_rows, slot_sem)
     expert = lax.broadcasted_iota(jnp.int32, (chip_rows, 1), 0) % slots // CAP
-
-    for twin_here in range(2):
-        rows = slot_rows[:, :, pl.ds(twin_here * slots, slots), :].reshape(chip_rows, rank)
+    half_rows = chip_rows // 2
+    halves = (pl.ds(0, half_rows), pl.ds(half_rows, half_rows))
+
+    def forward_half(twin_here):
+        def forward_near(step, carry):
+            y_from = lax.rem(y + y_count - near_order(step), y_count)
+            if twin_here == 0:
+                lax.fori_loop(4 * step - 4, 4 * step, make_pick, 0)
+            wait_bytes(near_rows.at[twin_here, y_from], near_sem.at[twin_here, y_from])
+            forward_rows(y_from, twin_here)
+            return carry
+
+        lax.fori_loop(1, y_count, forward_near, 0)
+
+    def hidden_half(twin_here):
+        wait_bytes(slot_rows.at[twin_here], slot_sem.at[twin_here])
+        rows = slot_rows[twin_here].reshape(chip_rows, rank)
         both_halves = jnp.zeros((chip_rows, gate_up.shape[5]), jnp.float32)
         for which in range(4):
             product = jnp.dot(
@@ -547,38 +564,60 @@
         gate, up = both_halves[:, :LANES], both_halves[:, LANES:]
         hidden = gate / (1.0 + jnp.exp(-gate)) * up * slot_weight[twin_here]
         hidden_all[x, y, twin_here] = hidden.astype(jnp.bfloat16)
-        held = hidden_all.at[x, y, twin_here]
 
         def hidden_near(step, carry):
-            if twin_here == 0:
-                device = {"dp": lax.rem(x + near_order(step), x_count)}
-            else:
-                device = {"seq": 2 * lax.rem(y + near_order(step), y_count) + c}
-            remote(held, held, sent.at[15], hid_sem.at[twin_here], device).start()
+            devices = (
+                {"dp": lax.rem(x + near_order(step), x_count)},
+                {"seq": 2 * lax.rem(y + near_order(step), y_count) + c},
+            )
+            for which in range(2):
+                held = hidden_all.at[x, y, twin_here, halves[which], :]
+                remote(held, held, sent.at[15], hid_sem.at[twin_here, which], devices[which]).start()
             return carry
 
         lax.fori_loop(1, x_count, hidden_near, 0)
 
+    def hidden_far(twin_here):
+        for which in range(2):
+            near = hidden_all.at[pl.ds(0, x_count - 1), 0, twin_here, halves[which], :]
+            wait_bytes(near, hid_sem.at[twin_here, which])
+
+            def push(step, carry):
+                if which == 0:
+                    held = hidden_all.at[:, y, twin_here, halves[0], :]
+                    device = {"seq": 2 * lax.rem(y + near_order(step), y_count) + c}
+                    remote(held, held, sent.at[16], hid_y_sem.at[twin_here, y], device).start()
+                else:
+                    held = hidden_all.at[x, :, twin_here, halves[1], :]
+                    device = {"dp": lax.rem(x + near_order(step), x_count)}
+                    remote(held, held, sent.at[18], hid_x_sem.at[twin_here, x], device).start()
+                return carry
+
+            lax.fori_loop(1, x_count, push, 0)
+
+    def hidden_wait(twin_here):
+        def arrive(step, carry):
+            y_from = lax.rem(y + y_count - near_order(step), y_count)
+            x_from = lax.rem(x + x_count - near_order(step), x_count)
+            wait_bytes(
+                hidden_all.at[:, y_from, twin_here, halves[0], :], hid_y_sem.at[twin_here, y_from]
+            )
+            wait_bytes(
+                hidden_all.at[x_from, :, twin_here, halves[1], :], hid_x_sem.at[twin_here, x_from]
+            )
+            return carry
+
+        lax.fori_loop(1, y_count, arrive, 0)
+
+    forward_half(0)
+    wait_bytes(gate_up.at[other_c], pair_g_sem)
+    hidden_half(0)
+    forward_half(1)
+    hidden_far(0)
+    hidden_half(1)
     ring_step(down_ring, 3)
     lax.fori_loop(4 * (y_count - 1), group, make_pick, 0)
-    wait_bytes(hidden_all.at[pl.ds(0, x_count - 1), y, 0], hid_sem.at[0])
-
-    def hidden_to_y(step, carry):
-        held = hidden_all.at[:, y, 0]
-        y_to = lax.rem(y + near_order(step), y_count)
-        remote(held, held, sent.at[16], hid_y_sem.at[y], {"seq": 2 * y_to + c}).start()
-        return carry
-
-    lax.fori_loop(1, y_count, hidden_to_y, 0)
-    wait_bytes(hidden_all.at[x, pl.ds(0, y_count - 1), 1], hid_sem.at[1])
-
-    def hidden_to_x(step, carry):
-        held = hidden_all.at[x, :, 1]
-        x_to = lax.rem(x + near_order(step), x_count)
-        remote(held, held, sent.at[18], hid_x_sem.at[x], {"dp": x_to}).start()
-        return carry
-
-    lax.fori_loop(1, x_count, hidden_to_x, 0)
+    hidden_far(1)
     ring_step(down_ring, half)
     wait_bytes(weights.at[other_c], pair_w_sem)
 
@@ -604,32 +643,14 @@
         to = pl.ds(pl.multiple_of((z_from * y_count + y_from) * slots, slots), slots)
         slot_out[:, to, :] = product.astype(jnp.bfloat16).reshape(group, slots, cols)
 
-    def down_step(step, carry):
-        y_from = lax.rem(y + y_count - near_order(step), y_count)
-        x_from = lax.rem(x + x_count - near_order(step), x_count)
-
-        @pl.when(step > 0)
-        def _arrive_y():
-            wait_bytes(hidden_all.at[:, y_from, 0], hid_y_sem.at[y_from])
-
-        def down_first(other, inner):
-            down_block(other, y_from, 0)
-            return inner
-
-        lax.fori_loop(0, x_count, down_first, 0)
-
-        @pl.when(step > 0)
-        def _arrive_x():
-            wait_bytes(hidden_all.at[x_from, :, 1], hid_x_sem.at[x_from])
-
-        def down_second(other, inner):
-            down_block(x_from, other, 1)
-            return inner
-
-        lax.fori_loop(0, y_count, down_second, 0)
-        return carry
-
-    lax.fori_loop(0, y_count, down_step, 0)
+    for twin_here in range(2):
+        hidden_wait(twin_here)
+
+        def down_one(chip, carry):
+            down_block(chip // y_count, chip % y_count, twin_here)
+            return carry
+
+        lax.fori_loop(0, group, down_one, 0)
 
     mine = x * y_count + y
 
@@ -712,7 +733,7 @@
     def _spread_done():
         wait_bytes(gate_up.at[0, pl.ds(0, z_count - 1), 0], sent.at[4])
 
-    wait_bytes(slot_rows.at[pl.ds(0, x_count - 1)], sent.at[5])
+    wait_bytes(slot_rows.at[:, pl.ds(0, x_count - 1)], sent.at[5])
     wait_bytes(info_x.at[pl.ds(0, x_count - 1)], sent.at[6])
     wait_bytes(weights.at[0, pl.ds(0, z_count - 1)], sent.at[7])
     wait_bytes(weights.at[0], sent.at[8])
@@ -722,9 +743,9 @@
     wait_bytes(out_rows, sent.at[12])
     wait_bytes(gate_up.at[0, pl.ds(0, z_count - 1)], sent.at[13])
     wait_bytes(gate_up.at[0], sent.at[14])
-    wait_bytes(hidden_all.at[pl.ds(0, 2), pl.ds(0, y_count - 1), 0], sent.at[15])
-    wait_bytes(hidden_all.at[:, pl.ds(0, y_count - 1), 0], sent.at[16])
-    wait_bytes(hidden_all.at[pl.ds(0, x_count - 1), :, 1], sent.at[18])
+    wait_bytes(hidden_all.at[pl.ds(0, x_count - 1), :, 0, halves[0], :], sent.at[15])
+    wait_bytes(hidden_all.at[pl.ds(0, x_count - 1), :, :, halves[0], :], sent.at[16])
+    wait_bytes(hidden_all.at[pl.ds(0, x_count - 1), :, :, halves[0], :], sent.at[18])
 
     @pl.when(y % 2 == c)
     def _whole_done():
@@ -784,9 +805,9 @@
             pltpu.VMEM((y_count, tok_rows, wide), bf16),
             pltpu.VMEM((y_count - 1, tok_rows, wide), bf16),
             pltpu.VMEM((y_count - 1, tok_rows, wide), bf16),
-            pltpu.VMEM((y_count - 1, z_count * slots, rank), bf16),
-            pltpu.VMEM((y_count, z_count * slots, rank), bf16),
-            pltpu.VMEM((x_count, y_count, 2 * slots, rank), bf16),
+            pltpu.VMEM((y_count - 1, 2, x_count * slots, rank), bf16),
+            pltpu.VMEM((2, y_count, x_count * slots, rank), bf16),
+            pltpu.VMEM((2, x_count, y_count, slots, rank), bf16),
             pltpu.VMEM(
                 (2, z_count, 2, experts_here, rank // z_count, 2 * hidden_cols), bf16
             ),
@@ -814,11 +835,11 @@
             dma((y_count,)),
             dma,
             dma,
-            dma((y_count,)),
-            dma,
+            dma((2, y_count)),
             dma((2,)),
-            dma((y_count,)),
-            dma((x_count,)),
+            dma((2, 2)),
+            dma((2, y_count)),
+            dma((2, x_count)),
             dma((group,)),
             dma((19,)),
         ],

time: 168 us -> 175 us (1.042)
  Pallas kernels: 165 us -> 172 us
    pallas_call x1, Pallas kernels: 165 us -> 172 us  [on_device(): pl.pallas_call(block_kernel, out_shape=jax.ShapeDtypeStruct((tok_rows, mo...]
where the time goes in v5:
time: 175 us; the launch traced here: 174 us
  Pallas kernels  172 us (98%)
  local copies, waits for them, and re-layouts  2.46 us (1%)
    pallas_call x1, Pallas kernels, on_device(): pl.pallas_call(block_kernel, out_shape=jax.ShapeDtypeStruct((tok_rows, mo...  172 us

profile of v5, /device:TPU:1, one launch (start us, length us, event | category | flops | bytes accessed | tf_op | source)
XLA Modules:
  0.0 174.5 jit_solution(9671222755825857390)
XLA Ops:
  0.0 172.0 %block.1 = bf16[128,5120]{1,0:T(8,128)(2,1)} custom-call(bf16[128,5120]{1,0:T(8,128)(2,1)} %query_ref.1, bf16[128,5120]{1,0:T(8,128)(2,1)} %key_ref.1, bf16[128,5120]{1,0:T(8,128)(2,1)} %value_ref.1, bf16[128,5120]{1,0:T(8,128)(2,1)} %stream_ref.1, bf16[2,128,5120]{2,1,0:T(8,128)(2,1)} %down_ref.1, bf16[2,1024,256]{2,1,0:T(8,128)(2,1)} %gate_up_ref.1, ...), custom_call_target="tpu_custom_call" | custom-call | tf_op jit(solution)/shard_map/block/pallas_call | solution.py:790
  172.0 2.5 %copy.14 = bf16[128,5120]{1,0:T(8,128)(2,1)} copy(bf16[128,5120]{1,0:T(8,128)(2,1)} %block.1) | data formatting | bytes 2621440

commit v6 on v4

--- a/solution.py
+++ b/solution.py
@@ -150,7 +150,7 @@
             kv_refs[which].at[:, my_cols], kv_in.at[which, my_rows, :], kv_sem
         ).start()
         pltpu.make_async_copy(
-            qs_refs[which].at[:, my_cols], qs_in.at[s, which], qs_sem.at[s]
+            qs_refs[which].at[:, my_cols], qs_in.at[s, which], qs_sem.at[which, s]
         ).start()
         pltpu.make_async_copy(
             down_ref.at[which, :, pl.ds(first_column(y), cols)],
@@ -234,24 +234,24 @@
 
 
     def send_batch(refs, slot_of, sem, send_sem, distances):
-        def one_copy(index, carry):
-            s_to = 2 * lax.rem(y + distances[0] + 2 * (index % len(distances)), y_count) + (
-                index // len(distances)
-            )
-            columns = pl.ds(pl.multiple_of(s_to * head_cols, head_cols), head_cols)
-            for which in range(2):
+        for which in range(2):
+
+            def one_copy(index, carry):
+                s_to = 2 * lax.rem(y + distances[0] + 2 * (index % len(distances)), y_count) + (
+                    index // len(distances)
+                )
+                columns = pl.ds(pl.multiple_of(s_to * head_cols, head_cols), head_cols)
                 remote(
-                    refs[which].at[:, columns], slot_of(which), send_sem, sem, {"seq": s_to}
+                    refs[which].at[:, columns], slot_of(which), send_sem, sem(which), {"seq": s_to}
                 ).start()
-            return carry
-
-        if len(distances) == 2:
-            columns = pl.ds(pl.multiple_of(pair * head_cols, head_cols), head_cols)
-            for which in range(2):
+                return carry
+
+            if len(distances) == 2:
+                columns = pl.ds(pl.multiple_of(pair * head_cols, head_cols), head_cols)
                 remote(
-                    refs[which].at[:, columns], slot_of(which), send_sem, sem, {"seq": pair}
+                    refs[which].at[:, columns], slot_of(which), send_sem, sem(which), {"seq": pair}
                 ).start()
-        lax.fori_loop(0, 2 * len(distances), one_copy, 0)
+            lax.fori_loop(0, 2 * len(distances), one_copy, 0)
 
     batches = ((1, 3), (2,))
 
@@ -259,7 +259,7 @@
         send_batch(
             kv_refs,
             lambda which: kv_in.at[which, my_rows, :],
-            kv_sem,
+            lambda which: kv_sem,
             batch_sem.at[0, batch],
             batches[batch],
         )
@@ -268,7 +268,7 @@
         send_batch(
             qs_refs,
             lambda which: qs_in.at[s, which],
-            qs_sem.at[s],
+            lambda which: qs_sem.at[which, s],
             batch_sem.at[1, batch],
             batches[batch],
         )
@@ -398,8 +398,12 @@
         def _previous():
             send_part(step - 1)
 
-        for core in range(2):
-            wait_bytes(qs_in.at[2 * y_from + core], qs_sem.at[2 * y_from + core])
+        def wait_rows(which):
+            for core in range(2):
+                s_from = 2 * y_from + core
+                wait_bytes(qs_in.at[s_from, which], qs_sem.at[which, s_from])
+
+        wait_rows(0)
         both = pl.ds(2 * y_from, 2)
         square = jnp.zeros((two, 1), jnp.float32)
         for head in range(heads_here):
@@ -416,6 +420,11 @@
             mixed = jnp.dot(raised, value_ones, preferred_element_type=jnp.float32)
             mixed = (mixed[:, :HEAD_DIM] / mixed[:, HEAD_DIM : HEAD_DIM + 1]).astype(jnp.bfloat16)
             att_out[both, :, part] = mixed.reshape(2, tok_rows, HEAD_DIM)
+
+        wait_rows(1)
+        for head in range(heads_here):
+            part = slice(head * HEAD_DIM, (head + 1) * HEAD_DIM)
+            mixed = att_out[both, :, part].reshape(two, HEAD_DIM)
             residual = qs_in[both, 1, :, part].reshape(two, HEAD_DIM).astype(
                 jnp.float32
             ) + gate_row[:, part] * mixed.astype(jnp.float32)
@@ -445,6 +454,7 @@
 
     lax.fori_loop(0, y_count, after_chip, 0)
     send_part(y_count - 1)
+    ring_step(down_ring, 2)
 
     def send_attended(index, carry):
         s_to = lax.rem(s + index, s_count)
@@ -509,7 +519,6 @@
 
     near_rows[y] = pick_rows(y)
     forward_rows(y)
-    ring_step(down_ring, 2)
 
     def forward_near(step, carry):
         y_from = lax.rem(y + y_count - near_order(step), y_count)
@@ -530,6 +539,7 @@
 
     lax.fori_loop(1, y_count, forward_near, 0)
 
+    ring_step(down_ring, 3)
     wait_bytes(gate_up.at[other_c], pair_g_sem)
     wait_bytes(slot_rows, slot_sem)
     expert = lax.broadcasted_iota(jnp.int32, (chip_rows, 1), 0) % slots // CAP
@@ -559,7 +569,6 @@
 
         lax.fori_loop(1, x_count, hidden_near, 0)
 
-    ring_step(down_ring, 3)
     lax.fori_loop(4 * (y_count - 1), group, make_pick, 0)
     wait_bytes(hidden_all.at[pl.ds(0, x_count - 1), y, 0], hid_sem.at[0])
 
@@ -801,7 +810,7 @@
             pltpu.VMEM((2, group * slots, 1), f32),
             pltpu.VMEM((group, tok_rows, group * 2 * slots), bf16),
             dma,
-            dma((s_count,)),
+            dma((2, s_count)),
             dma((2, 2)),
             dma,
             dma((2,)),

time: 168 us -> 169 us (level)
  no operation moved by 1% of the time
where the time goes in v6:
time: 169 us
  Pallas kernels  166 us (98%)
  local copies, waits for them, and re-layouts  2.46 us (1%)
    pallas_call x1, Pallas kernels, on_device(): pl.pallas_call(block_kernel, out_shape=jax.ShapeDtypeStruct((tok_rows, mo...  166 us

profile of v6, /device:TPU:1, one launch (start us, length us, event | category | flops | bytes accessed | tf_op | source)
XLA Modules:
  0.0 168.6 jit_solution(1451493457577065801)
XLA Ops:
  0.0 166.1 %block.1 = bf16[128,5120]{1,0:T(8,128)(2,1)} custom-call(bf16[128,5120]{1,0:T(8,128)(2,1)} %query_ref.1, bf16[128,5120]{1,0:T(8,128)(2,1)} %key_ref.1, bf16[128,5120]{1,0:T(8,128)(2,1)} %value_ref.1, bf16[128,5120]{1,0:T(8,128)(2,1)} %stream_ref.1, bf16[2,128,5120]{2,1,0:T(8,128)(2,1)} %down_ref.1, bf16[2,1024,256]{2,1,0:T(8,128)(2,1)} %gate_up_ref.1, ...), custom_call_target="tpu_custom_call" | custom-call | tf_op jit(solution)/shard_map/block/pallas_call | solution.py:778
  166.1 2.5 %copy.14 = bf16[128,5120]{1,0:T(8,128)(2,1)} copy(bf16[128,5120]{1,0:T(8,128)(2,1)} %block.1) | data formatting | bytes 2621440

commit v7 on v6

--- a/solution.py
+++ b/solution.py
@@ -278,6 +278,7 @@
         wait_bytes(qs_in.at[pl.ds(0, peers)], batch_sem.at[kind, batch])
 
     send_kv(0)
+    send_kv(1)
 
     always = z >= 0
     half = z_count // 2
@@ -333,16 +334,15 @@
 
     lax.fori_loop(1, x_count, info_to_x, 0)
     pass_on(*gate_ring, z, always, always)
-    send_kv(1)
-    ring_step(gate_ring, 1)
     wait_bytes(weights.at[c, z], near_w_sem)
     pass_on(*down_ring, z, always, always)
     batch_left(0, 0)
     send_qs(0)
+    ring_step(gate_ring, 1)
     ring_step(gate_ring, 2)
-    ring_step(gate_ring, 3)
     batch_left(0, 1)
     send_qs(1)
+    ring_step(gate_ring, 3)
 
     wait_bytes(info_x, info_sem.at[1])
     group = x_count * y_count
@@ -454,7 +454,6 @@
 
     lax.fori_loop(0, y_count, after_chip, 0)
     send_part(y_count - 1)
-    ring_step(down_ring, 2)
 
     def send_attended(index, carry):
         s_to = lax.rem(s + index, s_count)
@@ -519,6 +518,7 @@
 
     near_rows[y] = pick_rows(y)
     forward_rows(y)
+    ring_step(down_ring, 2)
 
     def forward_near(step, carry):
         y_from = lax.rem(y + y_count - near_order(step), y_count)
@@ -539,7 +539,6 @@
 
     lax.fori_loop(1, y_count, forward_near, 0)
 
-    ring_step(down_ring, 3)
     wait_bytes(gate_up.at[other_c], pair_g_sem)
     wait_bytes(slot_rows, slot_sem)
     expert = lax.broadcasted_iota(jnp.int32, (chip_rows, 1), 0) % slots // CAP
@@ -569,6 +568,7 @@
 
         lax.fori_loop(1, x_count, hidden_near, 0)
 
+    ring_step(down_ring, 3)
     lax.fori_loop(4 * (y_count - 1), group, make_pick, 0)
     wait_bytes(hidden_all.at[pl.ds(0, x_count - 1), y, 0], hid_sem.at[0])
 

time: 169 us -> 170 us (level)
  no operation moved by 1% of the time
where the time goes in v7:
time: 170 us
  Pallas kernels  167 us (98%)
  local copies, waits for them, and re-layouts  2.46 us (1%)
    pallas_call x1, Pallas kernels, on_device(): pl.pallas_call(block_kernel, out_shape=jax.ShapeDtypeStruct((tok_rows, mo...  167 us

profile of v7, /device:TPU:1, one launch (start us, length us, event | category | flops | bytes accessed | tf_op | source)
XLA Modules:
  0.0 169.6 jit_solution(16261086701033553339)
XLA Ops:
  0.0 167.1 %block.1 = bf16[128,5120]{1,0:T(8,128)(2,1)} custom-call(bf16[128,5120]{1,0:T(8,128)(2,1)} %query_ref.1, bf16[128,5120]{1,0:T(8,128)(2,1)} %key_ref.1, bf16[128,5120]{1,0:T(8,128)(2,1)} %value_ref.1, bf16[128,5120]{1,0:T(8,128)(2,1)} %stream_ref.1, bf16[2,128,5120]{2,1,0:T(8,128)(2,1)} %down_ref.1, bf16[2,1024,256]{2,1,0:T(8,128)(2,1)} %gate_up_ref.1, ...), custom_call_target="tpu_custom_call" | custom-call | tf_op jit(solution)/shard_map/block/pallas_call | solution.py:778
  167.2 2.5 %copy.14 = bf16[128,5120]{1,0:T(8,128)(2,1)} copy(bf16[128,5120]{1,0:T(8,128)(2,1)} %block.1) | data formatting | bytes 2621440

commit v8 on v6

--- a/solution.py
+++ b/solution.py
@@ -278,6 +278,7 @@
         wait_bytes(qs_in.at[pl.ds(0, peers)], batch_sem.at[kind, batch])
 
     send_kv(0)
+    send_kv(1)
 
     always = z >= 0
     half = z_count // 2
@@ -317,6 +318,8 @@
     gate_ring = (gate_up, ring_g_sem, sent.at[13], sent.at[14], pair_g_sem)
     down_ring = (weights, ring_sem, sent.at[7], sent.at[8], pair_w_sem)
 
+    wait_bytes(weights.at[c, z], near_w_sem)
+    pass_on(*down_ring, z, always, always)
     wait_bytes(gate_up.at[c, z], near_g_sem)
     wait_bytes(info_y, info_sem.at[0])
     pltpu.make_async_copy(info_y, info_x.at[x], info_sem.at[1]).start()
@@ -333,14 +336,8 @@
 
     lax.fori_loop(1, x_count, info_to_x, 0)
     pass_on(*gate_ring, z, always, always)
-    send_kv(1)
-    ring_step(gate_ring, 1)
-    wait_bytes(weights.at[c, z], near_w_sem)
-    pass_on(*down_ring, z, always, always)
     batch_left(0, 0)
     send_qs(0)
-    ring_step(gate_ring, 2)
-    ring_step(gate_ring, 3)
     batch_left(0, 1)
     send_qs(1)
 
@@ -443,17 +440,22 @@
         one_chip(step, carry)
 
         @pl.when(step == 0)
-        def _last_batch():
-            ring_step(gate_ring, half)
+        def _gate_one():
+            ring_step(gate_ring, 1)
+
+        @pl.when(step == 1)
+        def _down_one():
+            ring_step(down_ring, 1)
 
         @pl.when(step == 2)
-        def _ring_one():
-            ring_step(down_ring, 1)
+        def _gate_two():
+            ring_step(gate_ring, 2)
 
         return carry
 
     lax.fori_loop(0, y_count, after_chip, 0)
     send_part(y_count - 1)
+    ring_step(gate_ring, 3)
     ring_step(down_ring, 2)
 
     def send_attended(index, carry):
@@ -519,6 +521,7 @@
 
     near_rows[y] = pick_rows(y)
     forward_rows(y)
+    ring_step(gate_ring, half)
 
     def forward_near(step, carry):
         y_from = lax.rem(y + y_count - near_order(step), y_count)

time: 169 us -> 162 us (0.959)
  Pallas kernels: 166 us -> 160 us
    pallas_call x1, Pallas kernels: 166 us -> 160 us  [on_device(): pl.pallas_call(block_kernel, out_shape=jax.ShapeDtypeStruct((tok_rows, mo...]
where the time goes in v8:
time: 162 us
  Pallas kernels  160 us (99%)
  local copies, waits for them, and re-layouts  2.46 us (2%)
    pallas_call x1, Pallas kernels, on_device(): pl.pallas_call(block_kernel, out_shape=jax.ShapeDtypeStruct((tok_rows, mo...  160 us

profile of v8, /device:TPU:1, one launch (start us, length us, event | category | flops | bytes accessed | tf_op | source)
XLA Modules:
  0.0 162.2 jit_solution(5738436260794524748)
XLA Ops:
  0.0 159.7 %block.1 = bf16[128,5120]{1,0:T(8,128)(2,1)} custom-call(bf16[128,5120]{1,0:T(8,128)(2,1)} %query_ref.1, bf16[128,5120]{1,0:T(8,128)(2,1)} %key_ref.1, bf16[128,5120]{1,0:T(8,128)(2,1)} %value_ref.1, bf16[128,5120]{1,0:T(8,128)(2,1)} %stream_ref.1, bf16[2,128,5120]{2,1,0:T(8,128)(2,1)} %down_ref.1, bf16[2,1024,256]{2,1,0:T(8,128)(2,1)} %gate_up_ref.1, ...), custom_call_target="tpu_custom_call" | custom-call | tf_op jit(solution)/shard_map/block/pallas_call | solution.py:781
  159.8 2.5 %copy.14 = bf16[128,5120]{1,0:T(8,128)(2,1)} copy(bf16[128,5120]{1,0:T(8,128)(2,1)} %block.1) | data formatting | bytes 2621440

commit v9 on v8

--- a/solution.py
+++ b/solution.py
@@ -320,6 +320,8 @@
 
     wait_bytes(weights.at[c, z], near_w_sem)
     pass_on(*down_ring, z, always, always)
+    batch_left(0, 0)
+    send_qs(0)
     wait_bytes(gate_up.at[c, z], near_g_sem)
     wait_bytes(info_y, info_sem.at[0])
     pltpu.make_async_copy(info_y, info_x.at[x], info_sem.at[1]).start()
@@ -336,8 +338,6 @@
 
     lax.fori_loop(1, x_count, info_to_x, 0)
     pass_on(*gate_ring, z, always, always)
-    batch_left(0, 0)
-    send_qs(0)
     batch_left(0, 1)
     send_qs(1)
 
@@ -440,23 +440,23 @@
         one_chip(step, carry)
 
         @pl.when(step == 0)
+        def _down_one():
+            ring_step(down_ring, 1)
+
+        @pl.when(step == 1)
         def _gate_one():
             ring_step(gate_ring, 1)
 
-        @pl.when(step == 1)
-        def _down_one():
-            ring_step(down_ring, 1)
-
         @pl.when(step == 2)
-        def _gate_two():
-            ring_step(gate_ring, 2)
+        def _down_two():
+            ring_step(down_ring, 2)
 
         return carry
 
     lax.fori_loop(0, y_count, after_chip, 0)
     send_part(y_count - 1)
-    ring_step(gate_ring, 3)
-    ring_step(down_ring, 2)
+    ring_step(gate_ring, 2)
+    ring_step(down_ring, 3)
 
     def send_attended(index, carry):
         s_to = lax.rem(s + index, s_count)
@@ -521,7 +521,7 @@
 
     near_rows[y] = pick_rows(y)
     forward_rows(y)
-    ring_step(gate_ring, half)
+    ring_step(gate_ring, 3)
 
     def forward_near(step, carry):
         y_from = lax.rem(y + y_count - near_order(step), y_count)
@@ -542,7 +542,7 @@
 
     lax.fori_loop(1, y_count, forward_near, 0)
 
-    ring_step(down_ring, 3)
+    ring_step(gate_ring, half)
     wait_bytes(gate_up.at[other_c], pair_g_sem)
     wait_bytes(slot_rows, slot_sem)
     expert = lax.broadcasted_iota(jnp.int32, (chip_rows, 1), 0) % slots // CAP

time: 162 us -> 168 us (1.037)
  Pallas kernels: 160 us -> 165 us
    pallas_call x1, Pallas kernels: 160 us -> 165 us  [on_device(): pl.pallas_call(block_kernel, out_shape=jax.ShapeDtypeStruct((tok_rows, mo...]
where the time goes in v9:
time: 168 us; the launch traced here: 167 us
  Pallas kernels  165 us (98%)
  local copies, waits for them, and re-layouts  2.46 us (1%)
    pallas_call x1, Pallas kernels, on_device(): pl.pallas_call(block_kernel, out_shape=jax.ShapeDtypeStruct((tok_rows, mo...  165 us

profile of v9, /device:TPU:1, one launch (start us, length us, event | category | flops | bytes accessed | tf_op | source)
XLA Modules:
  0.0 167.0 jit_solution(141365441752326678)
XLA Ops:
  0.0 164.5 %block.1 = bf16[128,5120]{1,0:T(8,128)(2,1)} custom-call(bf16[128,5120]{1,0:T(8,128)(2,1)} %query_ref.1, bf16[128,5120]{1,0:T(8,128)(2,1)} %key_ref.1, bf16[128,5120]{1,0:T(8,128)(2,1)} %value_ref.1, bf16[128,5120]{1,0:T(8,128)(2,1)} %stream_ref.1, bf16[2,128,5120]{2,1,0:T(8,128)(2,1)} %down_ref.1, bf16[2,1024,256]{2,1,0:T(8,128)(2,1)} %gate_up_ref.1, ...), custom_call_target="tpu_custom_call" | custom-call | tf_op jit(solution)/shard_map/block/pallas_call | solution.py:781
  164.6 2.5 %copy.14 = bf16[128,5120]{1,0:T(8,128)(2,1)} copy(bf16[128,5120]{1,0:T(8,128)(2,1)} %block.1) | data formatting | bytes 2621440

commit v10 on v8

--- a/solution.py
+++ b/solution.py
@@ -456,7 +456,6 @@
     lax.fori_loop(0, y_count, after_chip, 0)
     send_part(y_count - 1)
     ring_step(gate_ring, 3)
-    ring_step(down_ring, 2)
 
     def send_attended(index, carry):
         s_to = lax.rem(s + index, s_count)
@@ -521,6 +520,7 @@
 
     near_rows[y] = pick_rows(y)
     forward_rows(y)
+    ring_step(down_ring, 2)
     ring_step(gate_ring, half)
 
     def forward_near(step, carry):
@@ -542,7 +542,6 @@
 
     lax.fori_loop(1, y_count, forward_near, 0)
 
-    ring_step(down_ring, 3)
     wait_bytes(gate_up.at[other_c], pair_g_sem)
     wait_bytes(slot_rows, slot_sem)
     expert = lax.broadcasted_iota(jnp.int32, (chip_rows, 1), 0) % slots // CAP
@@ -572,6 +571,7 @@
 
         lax.fori_loop(1, x_count, hidden_near, 0)
 
+    ring_step(down_ring, 3)
     lax.fori_loop(4 * (y_count - 1), group, make_pick, 0)
     wait_bytes(hidden_all.at[pl.ds(0, x_count - 1), y, 0], hid_sem.at[0])
 

time: 162 us -> 163 us (level)
  no operation moved by 1% of the time
where the time goes in v10:
time: 163 us; the launch traced here: 162 us
  Pallas kernels  160 us (98%)
  local copies, waits for them, and re-layouts  2.46 us (2%)
    pallas_call x1, Pallas kernels, on_device(): pl.pallas_call(block_kernel, out_shape=jax.ShapeDtypeStruct((tok_rows, mo...  160 us

profile of v10, /device:TPU:1, one launch (start us, length us, event | category | flops | bytes accessed | tf_op | source)
XLA Modules:
  0.0 162.2 jit_solution(4016210323842729099)
XLA Ops:
  0.0 159.7 %block.1 = bf16[128,5120]{1,0:T(8,128)(2,1)} custom-call(bf16[128,5120]{1,0:T(8,128)(2,1)} %query_ref.1, bf16[128,5120]{1,0:T(8,128)(2,1)} %key_ref.1, bf16[128,5120]{1,0:T(8,128)(2,1)} %value_ref.1, bf16[128,5120]{1,0:T(8,128)(2,1)} %stream_ref.1, bf16[2,128,5120]{2,1,0:T(8,128)(2,1)} %down_ref.1, bf16[2,1024,256]{2,1,0:T(8,128)(2,1)} %gate_up_ref.1, ...), custom_call_target="tpu_custom_call" | custom-call | tf_op jit(solution)/shard_map/block/pallas_call | solution.py:781
  159.7 2.5 %copy.14 = bf16[128,5120]{1,0:T(8,128)(2,1)} copy(bf16[128,5120]{1,0:T(8,128)(2,1)} %block.1) | data formatting | bytes 2621440
